TPU v7x, 512 devices: a whole 4x4x16 slice. The times are simulated.
512 devices in a mesh: group: 64 (over x, y, z_hi, core), tp: 8 (over z_lo).
Axes of the slice: x: 4, y: 4, z: 16 (z_hi: 2, z_lo: 8; z = z_hi * 8 + z_lo), core: 2. Of those that a mesh axis runs over, the one named last changes fastest.
Arguments:
- hidden: bfloat16 [4, 256, 5120], P(None, 'group', 'tp'), may hold values from -6 to 6
- queries: bfloat16 [4, 256, 8192], P(None, 'group', 'tp'), may hold values from -300 to 300
- stored_key_cache: bfloat16 [256, 1024, 1024], P('group', None, 'tp'), may hold values from -6 to 6
- stored_value_cache: bfloat16 [256, 1024, 1024], P('group', None, 'tp'), may hold values from -6 to 6
- lengths: int32 [256], P('group'), may hold values from 2 to 1024, as said below
- base_key_value_weight: bfloat16 [5120, 2048], P(None, 'tp'), may hold values from -0.078125 to 0.078125
- adapter_down_weight: bfloat16 [64, 5120], P('group', 'tp'), may hold values from -0.078125 to 0.078125
- adapter_up_weight: bfloat16 [64, 2048], P('group', 'tp'), may hold values from -0.75 to 0.75
- key_norm_gain: float32 [128], replicated, may hold values from 0.1 to 1.9
Outputs:
- attention: bfloat16 [4, 256, 8192], P(None, 'group', 'tp')
- new_entries: bfloat16 [4, 256, 2048], P(None, 'group', 'tp')
Inputs may be any that keep to these rules, and one draw needn't show every extreme that they name: `lengths`: in every block of 4 rows of one rollout group some row has exactly 1024 filled slots.
All inputs are finite; a program needn't handle non-finite values.
Results may differ from a plain program's by a relative error of at most 0.0055.
Values may be sent and summed in bfloat16 or wider, within the bound.
A program may use at most 64 MiB of HBM per device.

v0:
```python
import jax
import jax.numpy as jnp
from jax import lax
from jax.sharding import PartitionSpec as P

QH = 64
KVH = 8
HEAD = 128


adapter_scale = 2.0
norm_eps = 1e-06


def per_device(
    hidden,
    queries,
    stored_key_cache,
    stored_value_cache,
    lengths,
    base_key_value_weight,
    adapter_down_weight,
    adapter_up_weight,
    key_norm_gain,
):
    steps, rows, local_width = hidden.shape
    kv_local = base_key_value_weight.shape[1] // (2 * HEAD)
    groups = QH // KVH
    full_hidden = lax.all_gather(hidden, "tp", axis=2, tiled=True)
    flat = full_hidden.reshape(steps * rows, full_hidden.shape[2])
    widened_down_weight = lax.all_gather(adapter_down_weight, "tp", axis=1, tiled=True)
    full_a, full_b = (
        lax.all_gather(widened_down_weight, "group", axis=0, tiled=True),
        lax.all_gather(adapter_up_weight, "group", axis=0, tiled=True),
    )
    adapter_update = lax.dot_general(
        full_a, full_b, (((0,), (0,)), ((), ())), preferred_element_type=jnp.float32
    )
    merged_weight = base_key_value_weight.astype(jnp.float32) + adapter_scale * adapter_update
    projected = jnp.dot(flat.astype(jnp.float32), merged_weight, precision=lax.Precision.HIGHEST)
    projected = projected.reshape(steps, rows, kv_local, 2, HEAD)
    raw_keys = projected[:, :, :, 0, :]
    scale = lax.rsqrt(jnp.mean(raw_keys * raw_keys, axis=-1, keepdims=True) + norm_eps)
    new_keys = (raw_keys * scale * key_norm_gain).astype(jnp.bfloat16)
    new_values = projected[:, :, :, 1, :].astype(jnp.bfloat16)
    new_entries = jnp.stack([new_keys, new_values], axis=3).reshape(
        steps, rows, kv_local * 2 * HEAD
    )
    slots = stored_key_cache.shape[1]
    query_heads = queries.reshape(steps, rows, kv_local, groups, HEAD)
    keys_local = stored_key_cache.reshape(rows, slots, kv_local, HEAD)
    values_local = stored_value_cache.reshape(rows, slots, kv_local, HEAD)
    factor = HEAD ** (-0.5)
    cached = (
        jnp.einsum("srjgh,rcjh->srjgc", query_heads, keys_local, preferred_element_type=jnp.float32)
        * factor
    )
    valid = jnp.arange(slots, dtype=jnp.int32)[None, :] < lengths[:, None]
    cached = jnp.where(valid[None, :, None, None, :], cached, -jnp.inf)
    recent = (
        jnp.einsum("srjgh,trjh->srjgt", query_heads, new_keys, preferred_element_type=jnp.float32)
        * factor
    )
    causal = (
        jnp.arange(steps, dtype=jnp.int32)[None, :] <= jnp.arange(steps, dtype=jnp.int32)[:, None]
    )
    recent = jnp.where(causal[:, None, None, None, :], recent, -jnp.inf)
    top = jnp.maximum(
        jnp.max(cached, axis=-1, keepdims=True), jnp.max(recent, axis=-1, keepdims=True)
    )
    cached_exp = jnp.exp(cached - top)
    recent_exp = jnp.exp(recent - top)
    total = jnp.sum(cached_exp, axis=-1, keepdims=True) + jnp.sum(
        recent_exp, axis=-1, keepdims=True
    )
    cached_w = (cached_exp / total).astype(jnp.bfloat16)
    recent_w = (recent_exp / total).astype(jnp.bfloat16)
    result = jnp.einsum(
        "srjgc,rcjh->srjgh", cached_w, values_local, preferred_element_type=jnp.float32
    )
    result = result + jnp.einsum(
        "srjgt,trjh->srjgh", recent_w, new_values, preferred_element_type=jnp.float32
    )
    attention = result.reshape(steps, rows, kv_local * groups * HEAD).astype(jnp.bfloat16)
    return (attention, new_entries)


def solution(mesh):
    return jax.shard_map(
        per_device,
        mesh=mesh,
        in_specs=(
            P(None, "group", "tp"),
            P(None, "group", "tp"),
            P("group", None, "tp"),
            P("group", None, "tp"),
            P("group"),
            P(None, "tp"),
            P("group", "tp"),
            P("group", "tp"),
            P(),
        ),
        out_specs=(P(None, "group", "tp"), P(None, "group", "tp")),
        check_vma=False,
    )
```

profile of v0, /device:TPU:1, one launch (start us, length us, event | category | flops | bytes accessed | tf_op | source)
XLA Modules:
  0.0 420.1 jit_solution(16883925218499077331)
XLA Ops:
  0.6 0.0 copy-start
  0.6 0.0 copy-start.2
  0.7 43.6 %all_gather.12 = bf16[1,5120]{1,0:T(2,128)(2,1)S(1)} all-gather(bf16[1,640]{1,0:T(2,128)(2,1)} %param.15), channel_id=1, replica_groups=mesh['group'=64,'tp'=8] {'tp'}, dimensions={1}, use_global_device_ids=true | all-gather | bytes 11520 | tf_op jit(solution)/shard_map/all_gather | solution.py:31
  44.3 176.4 %all-gather = bf16[64,1,5120]{2,1,0:T(2,128)(2,1)S(1)} all-gather(bf16[1,1,5120]{2,1,0:T(2,128)(2,1)S(1)} %bitcast.82), channel_id=1, replica_groups=mesh['group'=64,'tp'=8] {'group'}, dimensions={0}, use_global_device_ids=true | all-gather | bytes 665600 | tf_op jit(solution)/shard_map/all_gather | solution.py:33
  220.6 146.5 %all-gather.1 = bf16[64,1,256]{2,1,0:T(2,128)(2,1)S(1)} all-gather(bf16[1,1,256]{2,1,0:T(2,128)(2,1)} %bitcast.84), channel_id=1, replica_groups=mesh['group'=64,'tp'=8] {'group'}, dimensions={0}, use_global_device_ids=true | all-gather | bytes 33280 | tf_op jit(solution)/shard_map/all_gather | solution.py:34
  367.2 5.0 %fusion = f32[5120,256]{1,0:T(8,128)} fusion(bf16[5120,256]{1,0:T(8,128)(2,1)} %param.14, bf16[64,1,5120]{2,1,0:T(2,128)(2,1)S(1)} %all-gather, bf16[64,1,256]{2,1,0:T(2,128)(2,1)S(1)} %all-gather.1), kind=kOutput, calls=%fused_computation.1 | convolution fusion | flops 171704320 | bytes 8552448 | tf_op jit(solution)/shard_map/dot_general | solution.py:36
  372.1 0.0 copy-done.2
  372.1 40.2 %all_gather.15 = bf16[4,4,5120]{2,1,0:T(4,128)(2,1)S(1)} all-gather(bf16[4,4,640]{2,1,0:T(4,128)(2,1)S(1)} %copy-done.2), channel_id=1, replica_groups=mesh['group'=64,'tp'=8] {'tp'}, dimensions={2}, use_global_device_ids=true | all-gather | bytes 184320 | tf_op jit(solution)/shard_map/all_gather | solution.py:29
  412.4 4.3 %convolution_bitcast_fusion.1 = f32[16,256]{1,0:T(8,128)S(1)} fusion(f32[5120,256]{1,0:T(8,128)} %fusion, bf16[16,5120]{1,0:T(8,128)(2,1)S(1)} %reshape.154), kind=kOutput, calls=%fused_computation.12 | convolution fusion | flops 251658240 | bytes 5423104 | tf_op jit(solution)/shard_map/dot_general | solution.py:40
  416.7 0.1 multiply_reduce_fusion
  416.8 0.0 copy-done.1
  416.9 0.0 copy-done.4
  416.9 0.3 fusion.30
  417.2 0.0 copy-done.3
  417.2 0.1 iota_compare_fusion
  417.3 0.0 copy-done
  417.3 0.5 fusion.29
  417.9 0.2 fusion.12
  418.1 0.0 copy-done.5
  418.1 0.3 convolution_bitcast_fusion
  418.5 0.2 fusion.5
  418.7 0.6 copy.27
  419.4 0.1 multiply_convert_fusion
  419.5 0.6 copy.63
  (17 shorter events, 0.2 us)
Async XLA Ops:
  0.6 416.6 %copy-start = (bf16[4,1024,128]{2,1,0:T(8,128)(2,1)S(1)}, bf16[4,1024,128]{2,1,0:T(8,128)(2,1)}, u32[]{:S(2)}) copy-start(bf16[4,1024,128]{2,1,0:T(8,128)(2,1)} %param.11) | copy-start | bytes 3145732
  0.6 371.5 %copy-start.2 = (bf16[4,4,640]{2,1,0:T(4,128)(2,1)S(1)}, bf16[4,4,640]{2,1,0:T(4,128)(2,1)}, u32[]{:S(2)}) copy-start(bf16[4,4,640]{2,1,0:T(4,128)(2,1)} %param.9) | copy-start | bytes 61444
  367.2 49.7 %copy-start.1 = (bf16[4,4,1024]{2,1,0:T(4,128)(2,1)S(1)}, bf16[4,4,1024]{2,1,0:T(4,128)(2,1)}, u32[]{:S(2)}) copy-start(bf16[4,4,1024]{2,1,0:T(4,128)(2,1)} %param.10) | copy-start | bytes 98308
  367.2 49.7 %copy-start.4 = (f32[128]{0:T(128)S(1)}, f32[128]{0:T(128)}, u32[]{:S(2)}) copy-start(f32[128]{0:T(128)} %param.17) | copy-start | bytes 1540
  367.2 50.0 %copy-start.3 = (s32[4]{0:T(128)S(1)}, s32[4]{0:T(128)}, u32[]{:S(2)}) copy-start(s32[4]{0:T(128)} %param.13) | copy-start | bytes 52
  372.1 46.0 %copy-start.5 = (bf16[4,1024,128]{2,1,0:T(8,128)(2,1)S(1)}, bf16[4,1024,128]{2,1,0:T(8,128)(2,1)}, u32[]{:S(2)}) copy-start(bf16[4,1024,128]{2,1,0:T(8,128)(2,1)} %param.12) | copy-start | bytes 3145732
where the time goes:
time: 422 us; the launch traced here: 420 us
  blocking collectives  407 us (96%)
  matrix products  10.7 us (3%)
    all_gather x1, blocking collectives, per_device(): lax.all_gather(widened_down_weight, 'group', axis=0, tiled=True)  176 us
    all_gather x1, blocking collectives, per_device(): lax.all_gather(adapter_up_weight, 'group', axis=0, tiled=True)  147 us
    all_gather x1, blocking collectives, per_device(): lax.all_gather(adapter_down_weight, 'tp', axis=1, tiled=True)  43.6 us
    all_gather x1, blocking collectives, per_device(): full_hidden = lax.all_gather(hidden, 'tp', axis=2, tiled=True)  40.2 us

commit v1 on v0

v1 whole, which is shorter than its diff:
```python
import functools

import jax
import jax.numpy as jnp
from jax import lax
from jax.experimental import pallas as pl
from jax.experimental.pallas import tpu as pltpu
from jax.sharding import PartitionSpec as P

HEAD = 128
STEPS = 4
ROWS = 4
HEADS = 8
TOKENS = STEPS * ROWS
QUERIES = STEPS * HEADS
TP = 8
PLANE = 32
KB = 5
UP = 3

ADAPTER_SCALE = 2.0
NORM_EPS = 1e-06
MESH = pl.DeviceIdType.MESH
BF = jnp.bfloat16
F32 = jnp.float32


def dot(a, b):
    return jnp.dot(a, b, preferred_element_type=F32)


def dot_t(a, b):
    return lax.dot_general(a, b, (((1,), (1,)), ((), ())), preferred_element_type=F32)


def kernel(
    hidden_hbm, queries_hbm, keys_hbm, values_hbm, lengths_hbm, weight_hbm, down_hbm, up_hbm, gain_hbm,
    att_ref, ent_ref,
    hidden_v, queries_v, keys_v, values_v, lengths_s, weight_v, down_v, up_v, gain_v,
    hf, q32, o32, tiles, hall, relay_up, relay_down, partner, bbuf, usend, urecv,
    loc_sem, kv_sem, tile_sem, hall_sem, relay_sem, partner_sem, b_sem, u_sem,
):
    g = lax.axis_index("group")
    t = lax.axis_index("tp")
    xy, zh, c = g // 4, (g // 2) % 2, g % 2
    z = zh * 8 + t
    me = xy * 2 + c

    def at_z(where):
        where = where % 16
        return (xy * 4 + (where // 8) * 2 + c, where % 8)

    def in_plane(i):
        p = (me + 1 + i) % PLANE
        return ((p // 2) * 4 + zh * 2 + p % 2, t)

    def remote(src, dst, send, recv, to):
        return pltpu.make_async_remote_copy(
            src_ref=src, dst_ref=dst, send_sem=send, recv_sem=recv, device_id=to, device_id_type=MESH
        )

    def wait_bytes(ref, sem):
        pltpu.make_async_copy(ref, ref, sem).wait()

    small = [
        pltpu.make_async_copy(src, dst, loc_sem.at[i])
        for i, (src, dst) in enumerate(
            (
                (hidden_hbm, hidden_v),
                (down_hbm, down_v),
                (up_hbm, up_v),
                (queries_hbm, queries_v),
                (lengths_hbm, lengths_s),
                (gain_hbm, gain_v),
                (weight_hbm, weight_v),
            )
        )
    ]
    for copy in small[:6]:
        copy.start()
    barrier = pltpu.get_barrier_semaphore()

    def greet_plane(i, _):
        pl.semaphore_signal(barrier, inc=1, device_id=in_plane(i), device_id_type=MESH)
        return 0

    lax.fori_loop(0, PLANE - 1, greet_plane, 0)

    def greet_z(i, _):
        pl.semaphore_signal(barrier, inc=1, device_id=at_z(z + 1 + i), device_id_type=MESH)
        pl.semaphore_signal(barrier, inc=1, device_id=at_z(z + 15 - i), device_id_type=MESH)
        return 0

    lax.fori_loop(0, 4, greet_z, 0)

    kv = []
    for r in range(ROWS):
        kv.append(
            (
                pltpu.make_async_copy(keys_hbm.at[r], keys_v.at[r], kv_sem.at[0, r]),
                pltpu.make_async_copy(values_hbm.at[r], values_v.at[r], kv_sem.at[1, r]),
            )
        )
        kv[r][0].start()
        kv[r][1].start()
    small[6].start()

    small[0].wait()
    for s in range(STEPS):
        hf[s * ROWS : (s + 1) * ROWS, :] = hidden_v[s].astype(F32)
    for k in range(KB):
        hall[t, k] = hf[:, k * HEAD : (k + 1) * HEAD].astype(BF)
    small[1].wait()
    small[2].wait()
    down = down_v[...].astype(F32)
    up = up_v[...].astype(F32)
    for k in range(KB):
        tiles[me, k : k + 1, :] = down[:, k * HEAD : (k + 1) * HEAD]
    for k in range(2):
        tiles[me, KB + k : KB + k + 1, :] = up[:, k * HEAD : (k + 1) * HEAD]
    tiles[me, 7:8, :] = jnp.zeros((1, HEAD), F32)

    pl.semaphore_wait(barrier, PLANE - 1 + 8)

    first_up = remote(hall.at[t, pl.ds(0, UP)], relay_up, relay_sem.at[0, 0], relay_sem.at[0, 1], at_z(z + 4))
    first_down = remote(
        hall.at[t, pl.ds(UP, KB - UP)], relay_down, relay_sem.at[1, 0], relay_sem.at[1, 1], at_z(z + 12)
    )
    first_up.start()
    first_down.start()

    def send_tile(i, _):
        remote(tiles.at[me], tiles.at[me], tile_sem.at[0], tile_sem.at[1], in_plane(i)).start()
        return 0

    lax.fori_loop(0, PLANE - 1, send_tile, 0)

    def send_hidden(d):
        @pl.when(t + d < TP)
        def _():
            remote(hall.at[t], hall.at[t], hall_sem.at[0], hall_sem.at[1], (g, t + d)).start()

        @pl.when(t >= d)
        def _():
            remote(hall.at[t], hall.at[t], hall_sem.at[0], hall_sem.at[1], (g, t - d)).start()

    for d in range(1, 5):
        send_hidden(d)

    small[3].wait()
    for s in range(STEPS):
        for h in range(HEADS):
            q32[pl.ds(s * HEADS + h, ROWS, stride=QUERIES), :] = queries_v[
                s, :, h * HEAD : (h + 1) * HEAD
            ].astype(F32)
    small[4].wait()
    factor = HEAD ** (-0.5)

    def cached(r):
        kv[r][0].wait()
        q = q32[r * QUERIES : (r + 1) * QUERIES, :].astype(BF)
        scores = dot_t(q, keys_v[r]) * factor
        slot = lax.broadcasted_iota(jnp.int32, scores.shape, 1)
        scores = jnp.where(slot < lengths_s[r], scores, -jnp.inf)
        top = jnp.max(scores, axis=1, keepdims=True)
        p = jnp.exp(scores - top)
        total = jnp.sum(p, axis=1, keepdims=True)
        kv[r][1].wait()
        return top, total, dot(p.astype(BF), values_v[r])

    rows = [cached(0), cached(1)]

    first_up.wait_recv()
    second_up = remote(relay_up, partner.at[pl.ds(0, UP)], partner_sem.at[0, 0], partner_sem.at[0, 1], at_z(z + 4))
    second_up.start()
    first_down.wait_recv()
    second_down = remote(
        relay_down, partner.at[pl.ds(UP, KB - UP)], partner_sem.at[1, 0], partner_sem.at[1, 1], at_z(z + 12)
    )
    second_down.start()
    for d in range(5, 8):
        send_hidden(d)

    rows += [cached(2), cached(3)]

    wait_bytes(tiles.at[pl.ds(0, PLANE - 1)], tile_sem.at[1])
    a = []
    for k in range(KB):
        block = tiles_rows(tiles, k)
        a.append(jnp.concatenate([block] * 4, axis=0))
    a = jnp.concatenate(a, axis=1)
    bbuf[0, :, 0:HEAD] = tiles_rows(tiles, KB)
    bbuf[0, :, HEAD : 2 * HEAD] = tiles_rows(tiles, KB + 1)
    send_b = remote(bbuf.at[0], bbuf.at[1], b_sem.at[0], b_sem.at[1], at_z(z + 8))
    send_b.start()

    def parts(blocks):
        u = dot_t(jnp.concatenate(blocks, axis=1), a)
        high = u.astype(BF).astype(F32)
        rest = u - high
        mid = rest.astype(BF).astype(F32)
        low = (rest - mid).astype(BF).astype(F32)
        lane = lax.broadcasted_iota(jnp.int32, u.shape, 1)
        zero = jnp.zeros_like(u)
        packed = jnp.where(lane < 32, high, jnp.where(lane < 64, mid, jnp.where(lane < 96, low, zero)))
        return packed.astype(BF)

    urecv[0, t] = parts([hall[t, k] for k in range(KB)])

    def send_own(i, _):
        remote(urecv.at[0, t], urecv.at[0, t], u_sem.at[0, 0], u_sem.at[0, 1], (g, (t + 1 + i) % TP)).start()
        return 0

    lax.fori_loop(0, TP - 1, send_own, 0)

    second_up.wait_recv()
    second_down.wait_recv()
    usend[...] = parts([partner[k] for k in range(KB)])
    other = xy * 4 + (1 - zh) * 2 + c

    def send_cross(i, _):
        remote(usend, urecv.at[1, t], u_sem.at[1, 0], u_sem.at[1, 1], (other, (t + i) % TP)).start()
        return 0

    lax.fori_loop(0, TP, send_cross, 0)

    wait_bytes(hall.at[pl.ds(0, TP - 1)], hall_sem.at[1])
    small[6].wait()
    base = jnp.zeros((TOKENS, 2 * HEAD), F32)
    for i in range(TP):
        block = jnp.concatenate([hall[i, k] for k in range(KB)], axis=1)
        base = base + dot(block, weight_v[i * KB * HEAD : (i + 1) * KB * HEAD, :])

    top_c = jnp.concatenate([r[0] for r in rows], axis=0)
    total_c = jnp.concatenate([r[1] for r in rows], axis=0)
    acc_c = jnp.concatenate([r[2] for r in rows], axis=0)
    small[5].wait()
    gain = gain_v[...].reshape(1, HEAD)

    send_b.wait_recv()
    b_own = jnp.concatenate([bbuf[0]] * 4, axis=0)
    b_other = jnp.concatenate([bbuf[1]] * 4, axis=0)
    wait_bytes(urecv.at[0, pl.ds(0, TP - 1)], u_sem.at[0, 1])
    update = dot(urecv[0].reshape(TP * TOKENS, HEAD), b_own)
    wait_bytes(urecv.at[1], u_sem.at[1, 1])
    update = update + dot(urecv[1].reshape(TP * TOKENS, HEAD), b_other)
    update = jnp.sum(update.reshape(TP, TOKENS, 2 * HEAD), axis=0)
    projected = base + ADAPTER_SCALE * update

    raw = projected[:, 0:HEAD]
    value = projected[:, HEAD : 2 * HEAD]
    scale = lax.rsqrt(jnp.mean(raw * raw, axis=1, keepdims=True) + NORM_EPS)
    key = raw * scale * gain
    for s in range(STEPS):
        ent_ref[s, :, 0:HEAD] = key[s * ROWS : (s + 1) * ROWS].astype(BF)
        ent_ref[s, :, HEAD : 2 * HEAD] = value[s * ROWS : (s + 1) * ROWS].astype(BF)

    scores = dot_t(q32[...].astype(BF), key.astype(BF)) * factor
    qi = lax.broadcasted_iota(jnp.int32, scores.shape, 0)
    ki = lax.broadcasted_iota(jnp.int32, scores.shape, 1)
    seen = (ki % ROWS == qi // QUERIES) & (ki // ROWS <= (qi % QUERIES) // HEADS)
    scores = jnp.where(seen, scores, -jnp.inf)
    top = jnp.maximum(top_c, jnp.max(scores, axis=1, keepdims=True))
    p = jnp.exp(scores - top)
    carry = jnp.exp(top_c - top)
    total = carry * total_c + jnp.sum(p, axis=1, keepdims=True)
    result = (carry * acc_c + dot(p.astype(BF), value.astype(BF))) / total
    o32[...] = result
    for s in range(STEPS):
        for h in range(HEADS):
            att_ref[s, :, h * HEAD : (h + 1) * HEAD] = o32[
                pl.ds(s * HEADS + h, ROWS, stride=QUERIES), :
            ].astype(BF)

    first_up.wait_send()
    first_down.wait_send()
    second_up.wait_send()
    second_down.wait_send()
    send_b.wait_send()
    wait_bytes(tiles.at[pl.ds(0, PLANE - 1)], tile_sem.at[0])
    wait_bytes(hall.at[pl.ds(0, TP - 1)], hall_sem.at[0])
    wait_bytes(urecv.at[0, pl.ds(0, TP - 1)], u_sem.at[0, 0])
    wait_bytes(urecv.at[1], u_sem.at[1, 0])


def tiles_rows(tiles, k):
    return tiles[:, k, :].astype(BF)


def per_device(hidden, queries, keys, values, lengths, weight, down, up, gain):
    slots = keys.shape[1]
    dma = pltpu.SemaphoreType.DMA
    return pl.pallas_call(
        kernel,
        name="decode",
        out_shape=(
            jax.ShapeDtypeStruct(queries.shape, BF),
            jax.ShapeDtypeStruct((STEPS, ROWS, 2 * HEAD), BF),
        ),
        in_specs=[pl.BlockSpec(memory_space=pl.ANY)] * 9,
        out_specs=(pl.BlockSpec(memory_space=pltpu.VMEM),) * 2,
        scratch_shapes=[
            pltpu.VMEM(hidden.shape, BF),
            pltpu.VMEM(queries.shape, BF),
            pltpu.VMEM(keys.shape, BF),
            pltpu.VMEM(values.shape, BF),
            pltpu.SMEM(lengths.shape, jnp.int32),
            pltpu.VMEM(weight.shape, BF),
            pltpu.VMEM(down.shape, BF),
            pltpu.VMEM(up.shape, BF),
            pltpu.VMEM(gain.shape, F32),
            pltpu.VMEM((TOKENS, KB * HEAD), F32),
            pltpu.VMEM((ROWS * QUERIES, HEAD), F32),
            pltpu.VMEM((ROWS * QUERIES, HEAD), F32),
            pltpu.VMEM((PLANE, 8, HEAD), F32),
            pltpu.VMEM((TP, KB, TOKENS, HEAD), BF),
            pltpu.VMEM((UP, TOKENS, HEAD), BF),
            pltpu.VMEM((KB - UP, TOKENS, HEAD), BF),
            pltpu.VMEM((KB, TOKENS, HEAD), BF),
            pltpu.VMEM((2, PLANE, 2 * HEAD), BF),
            pltpu.VMEM((TOKENS, HEAD), BF),
            pltpu.VMEM((2, TP, TOKENS, HEAD), BF),
            dma((7,)),
            dma((2, ROWS)),
            dma((2,)),
            dma((2,)),
            dma((2, 2)),
            dma((2, 2)),
            dma((2,)),
            dma((2, 2)),
        ],
        compiler_params=pltpu.CompilerParams(
            collective_id=0, has_side_effects=True, vmem_limit_bytes=32 * 1024 * 1024
        ),
    )(hidden, queries, keys, values, lengths, weight, down, up, gain)


def solution(mesh):
    return jax.shard_map(
        per_device,
        mesh=mesh,
        in_specs=(
            P(None, "group", "tp"),
            P(None, "group", "tp"),
            P("group", None, "tp"),
            P("group", None, "tp"),
            P("group"),
            P(None, "tp"),
            P("group", "tp"),
            P("group", "tp"),
            P(),
        ),
        out_specs=(P(None, "group", "tp"), P(None, "group", "tp")),
        check_vma=False,
    )
```

time: 422 us -> 47.7 us (0.11)
  blocking collectives: 407 us -> 0 us
  Pallas kernels: 0 us -> 37.1 us
  matrix products: 10.7 us -> 0 us
  local copies, waits for them, and re-layouts: 1.38 us -> 9.55 us
    all_gather x4 -> x0, blocking collectives: 407 us -> none  [the longest x1 176 us: per_device(): lax.all_gather(widened_down_weight, 'group', axis=0, tiled=True)]
    pallas_call x0 -> x1, Pallas kernels: none -> 37.1 us  [per_device(): pl.pallas_call(kernel, name='decode', out_shape=(jax.ShapeDtypeStruct(que...]
    dot_general x6 -> x0, matrix products: 10.7 us -> none  [the longest x1 4.98 us: per_device(): lax.dot_general(full_a, full_b, (((0,), (0,)), ((), ())), preferred_eleme...]
    unnamed x14 -> x20, local copies, waits for them, and re-layouts: 0.67 us -> 9.55 us
where the time goes in v1:
time: 47.7 us; the launch traced here: 47.3 us
  Pallas kernels  37.1 us (78%)
  local copies, waits for them, and re-layouts  9.55 us (20%)
  between operations  0.66 us (1%)
    pallas_call x1, Pallas kernels, per_device(): pl.pallas_call(kernel, name='decode', out_shape=(jax.ShapeDtypeStruct(que...  37.1 us
    unnamed x20, local copies, waits for them, and re-layouts  9.55 us

profile of v1, /device:TPU:1, one launch (start us, length us, event | category | flops | bytes accessed | tf_op | source)
XLA Modules:
  0.0 47.3 jit_solution(1957429699321326244)
XLA Ops:
  0.6 0.0 copy-start
  0.6 1.7 %copy-done = bf16[5120,256]{1,0:T(8,128)(2,1)S(1)} copy-done((bf16[5120,256]{1,0:T(8,128)(2,1)S(1)}, bf16[5120,256]{1,0:T(8,128)(2,1)}, u32[]{:S(2)}) %copy-start) | copy-done | bytes 2621464
  2.4 0.0 copy-start.1
  2.4 1.2 %copy-done.1 = bf16[4,1024,128]{2,1,0:T(8,128)(2,1)S(1)} copy-done((bf16[4,1024,128]{2,1,0:T(8,128)(2,1)S(1)}, bf16[4,1024,128]{2,1,0:T(8,128)(2,1)}, u32[]{:S(2)}) %copy-start.1) | copy-done | bytes 1048600
  3.6 0.0 copy-start.2
  3.6 1.2 %copy-done.2 = bf16[4,1024,128]{2,1,0:T(8,128)(2,1)S(1)} copy-done((bf16[4,1024,128]{2,1,0:T(8,128)(2,1)S(1)}, bf16[4,1024,128]{2,1,0:T(8,128)(2,1)}, u32[]{:S(2)}) %copy-start.2) | copy-done | bytes 1048600
  4.8 0.0 copy-start.3
  4.8 0.8 %copy-done.3 = bf16[4,4,1024]{2,1,0:T(4,128)(2,1)S(1)} copy-done((bf16[4,4,1024]{2,1,0:T(4,128)(2,1)S(1)}, bf16[4,4,1024]{2,1,0:T(4,128)(2,1)}, u32[]{:S(2)}) %copy-start.3) | copy-done | bytes 32792
  5.6 0.0 copy-start.4
  5.6 0.7 %copy-done.4 = bf16[4,4,640]{2,1,0:T(4,128)(2,1)S(1)} copy-done((bf16[4,4,640]{2,1,0:T(4,128)(2,1)S(1)}, bf16[4,4,640]{2,1,0:T(4,128)(2,1)}, u32[]{:S(2)}) %copy-start.4) | copy-done | bytes 20504
  6.3 0.0 copy-start.5
  6.3 0.7 %copy-done.5 = bf16[1,640]{1,0:T(2,128)(2,1)S(1)} copy-done((bf16[1,640]{1,0:T(2,128)(2,1)S(1)}, bf16[1,640]{1,0:T(2,128)(2,1)}, u32[]{:S(2)}) %copy-start.5) | copy-done | bytes 1304
  7.0 0.0 copy-start.6
  7.0 0.7 %copy-done.6 = bf16[1,256]{1,0:T(2,128)(2,1)S(1)} copy-done((bf16[1,256]{1,0:T(2,128)(2,1)S(1)}, bf16[1,256]{1,0:T(2,128)(2,1)}, u32[]{:S(2)}) %copy-start.6) | copy-done | bytes 536
  7.7 0.0 copy-start.7
  7.7 0.7 %copy-done.7 = s32[4]{0:T(128)S(1)} copy-done((s32[4]{0:T(128)S(1)}, s32[4]{0:T(128)}, u32[]{:S(2)}) %copy-start.7) | copy-done | bytes 40
  8.3 0.0 copy-start.8
  8.3 0.7 %copy-done.8 = f32[128]{0:T(128)S(1)} copy-done((f32[128]{0:T(128)S(1)}, f32[128]{0:T(128)}, u32[]{:S(2)}) %copy-start.8) | copy-done | bytes 536
  9.0 37.1 %decode.1 = (bf16[4,4,1024]{2,1,0:T(4,128)(2,1)S(1)}, bf16[4,4,256]{2,1,0:T(4,128)(2,1)S(1)}) custom-call(bf16[4,4,640]{2,1,0:T(4,128)(2,1)S(1)} %copy-done.4, bf16[4,4,1024]{2,1,0:T(4,128)(2,1)S(1)} %copy-done.3, bf16[4,1024,128]{2,1,0:T(8,128)(2,1)S(1)} %copy-done.1, bf16[4,1024,128]{2,1,0:T(8,128)(2,1)S(1)} %copy-done.2, s32[4]{0:T(128)S(1)} %copy-done.7, ...), custom_call_target="tpu_custom_call" | custom-call | tf_op jit(solution)/shard_map/decode/pallas_call | solution.py:293
  46.1 0.6 %copy.13 = bf16[4,4,1024]{2,1,0:T(4,128)(2,1)} copy(bf16[4,4,1024]{2,1,0:T(4,128)(2,1)S(1)} %get-tuple-element.4) | data formatting | bytes 65536
  46.7 0.6 %copy.14 = bf16[4,4,256]{2,1,0:T(4,128)(2,1)} copy(bf16[4,4,256]{2,1,0:T(4,128)(2,1)S(1)} %get-tuple-element.5) | data formatting | bytes 16384
Async XLA Ops:
  0.6 1.7 %copy-start = (bf16[5120,256]{1,0:T(8,128)(2,1)S(1)}, bf16[5120,256]{1,0:T(8,128)(2,1)}, u32[]{:S(2)}) copy-start(bf16[5120,256]{1,0:T(8,128)(2,1)} %weight_hbm.1) | copy-start | bytes 7864324
  2.4 1.2 %copy-start.1 = (bf16[4,1024,128]{2,1,0:T(8,128)(2,1)S(1)}, bf16[4,1024,128]{2,1,0:T(8,128)(2,1)}, u32[]{:S(2)}) copy-start(bf16[4,1024,128]{2,1,0:T(8,128)(2,1)} %keys_hbm.1) | copy-start | bytes 3145732
  3.6 1.2 %copy-start.2 = (bf16[4,1024,128]{2,1,0:T(8,128)(2,1)S(1)}, bf16[4,1024,128]{2,1,0:T(8,128)(2,1)}, u32[]{:S(2)}) copy-start(bf16[4,1024,128]{2,1,0:T(8,128)(2,1)} %values_hbm.1) | copy-start | bytes 3145732
  4.8 0.8 %copy-start.3 = (bf16[4,4,1024]{2,1,0:T(4,128)(2,1)S(1)}, bf16[4,4,1024]{2,1,0:T(4,128)(2,1)}, u32[]{:S(2)}) copy-start(bf16[4,4,1024]{2,1,0:T(4,128)(2,1)} %queries_hbm.1) | copy-start | bytes 98308
  5.6 0.7 %copy-start.4 = (bf16[4,4,640]{2,1,0:T(4,128)(2,1)S(1)}, bf16[4,4,640]{2,1,0:T(4,128)(2,1)}, u32[]{:S(2)}) copy-start(bf16[4,4,640]{2,1,0:T(4,128)(2,1)} %hidden_hbm.1) | copy-start | bytes 61444
  6.3 0.7 %copy-start.5 = (bf16[1,640]{1,0:T(2,128)(2,1)S(1)}, bf16[1,640]{1,0:T(2,128)(2,1)}, u32[]{:S(2)}) copy-start(bf16[1,640]{1,0:T(2,128)(2,1)} %down_hbm.1) | copy-start | bytes 3844
  7.0 0.7 %copy-start.6 = (bf16[1,256]{1,0:T(2,128)(2,1)S(1)}, bf16[1,256]{1,0:T(2,128)(2,1)}, u32[]{:S(2)}) copy-start(bf16[1,256]{1,0:T(2,128)(2,1)} %up_hbm.1) | copy-start | bytes 1540
  7.7 0.7 %copy-start.7 = (s32[4]{0:T(128)S(1)}, s32[4]{0:T(128)}, u32[]{:S(2)}) copy-start(s32[4]{0:T(128)} %lengths_hbm.1) | copy-start | bytes 52
  8.3 0.7 %copy-start.8 = (f32[128]{0:T(128)S(1)}, f32[128]{0:T(128)}, u32[]{:S(2)}) copy-start(f32[128]{0:T(128)} %gain_hbm.1) | copy-start | bytes 1540

commit v2 on v1

--- a/solution.py
+++ b/solution.py
@@ -297,7 +297,7 @@
             jax.ShapeDtypeStruct(queries.shape, BF),
             jax.ShapeDtypeStruct((STEPS, ROWS, 2 * HEAD), BF),
         ),
-        in_specs=[pl.BlockSpec(memory_space=pl.ANY)] * 9,
+        in_specs=[pl.BlockSpec(memory_space=pltpu.HBM)] * 9,
         out_specs=(pl.BlockSpec(memory_space=pltpu.VMEM),) * 2,
         scratch_shapes=[
             pltpu.VMEM(hidden.shape, BF),
@@ -330,7 +330,7 @@
             dma((2, 2)),
         ],
         compiler_params=pltpu.CompilerParams(
-            collective_id=0, has_side_effects=True, vmem_limit_bytes=32 * 1024 * 1024
+            collective_id=0, has_side_effects=True, vmem_limit_bytes=60 * 1024 * 1024
         ),
     )(hidden, queries, keys, values, lengths, weight, down, up, gain)
 

time: 47.7 us -> 41.2 us (0.86)
  local copies, waits for them, and re-layouts: 9.55 us -> 2.68 us
  Pallas kernels: 37.1 us -> 37.6 us
    unnamed x20 -> x2, local copies, waits for them, and re-layouts: 9.55 us -> 2.68 us
    pallas_call x1, Pallas kernels: 37.1 us -> 37.6 us  [per_device(): pl.pallas_call(kernel, name='decode', out_shape=(jax.ShapeDtypeStruct(que...]
where the time goes in v2:
time: 41.2 us; the launch traced here: 41 us
  Pallas kernels  37.6 us (91%)
  local copies, waits for them, and re-layouts  2.68 us (7%)
  between operations  0.64 us (2%)
    pallas_call x1, Pallas kernels, per_device(): pl.pallas_call(kernel, name='decode', out_shape=(jax.ShapeDtypeStruct(que...  37.6 us
    unnamed x2, local copies, waits for them, and re-layouts  2.68 us

profile of v2, /device:TPU:1, one launch (start us, length us, event | category | flops | bytes accessed | tf_op | source)
XLA Modules:
  0.0 41.0 jit_solution(3161160822775671836)
XLA Ops:
  0.6 37.6 %decode.1 = (bf16[4,4,1024]{2,1,0:T(4,128)(2,1)}, bf16[4,4,256]{2,1,0:T(4,128)(2,1)}) custom-call(bf16[4,4,640]{2,1,0:T(4,128)(2,1)} %hidden_hbm.1, bf16[4,4,1024]{2,1,0:T(4,128)(2,1)} %queries_hbm.1, bf16[4,1024,128]{2,1,0:T(8,128)(2,1)} %keys_hbm.1, bf16[4,1024,128]{2,1,0:T(8,128)(2,1)} %values_hbm.1, s32[4]{0:T(128)} %lengths_hbm.1, ...), custom_call_target="tpu_custom_call" | custom-call | tf_op jit(solution)/shard_map/decode/pallas_call | solution.py:293
  38.3 1.4 %copy.13 = bf16[4,4,1024]{2,1,0:T(4,128)(2,1)} copy(bf16[4,4,1024]{2,1,0:T(4,128)(2,1)} %get-tuple-element.4) | data formatting | bytes 65536
  39.7 1.3 %copy.14 = bf16[4,4,256]{2,1,0:T(4,128)(2,1)} copy(bf16[4,4,256]{2,1,0:T(4,128)(2,1)} %get-tuple-element.5) | data formatting | bytes 16384

commit v3 on v2

v3 whole, which is shorter than its diff:
```python
import jax
import jax.numpy as jnp
from jax import lax
from jax.experimental import pallas as pl
from jax.experimental.pallas import tpu as pltpu
from jax.sharding import PartitionSpec as P

HEAD = 128
STEPS = 4
ROWS = 4
HEADS = 8
TOKENS = STEPS * ROWS
QUERIES = STEPS * HEADS
TP = 8
PLANE = 32
KB = 5

ADAPTER_SCALE = 2.0
NORM_EPS = 1e-06
MESH = pl.DeviceIdType.MESH
BF = jnp.bfloat16
F32 = jnp.float32


def dot(a, b):
    return jnp.dot(a, b, preferred_element_type=F32)


def dot_t(a, b):
    return lax.dot_general(a, b, (((1,), (1,)), ((), ())), preferred_element_type=F32)


def kernel(
    hidden_hbm, queries_hbm, keys_hbm, values_hbm, lengths_hbm, weight_hbm, down_hbm, up_hbm, gain_hbm,
    att_ref, ent_ref,
    hidden_v, queries_v, keys_v, values_v, lengths_s, weight_v, down_v, up_v, gain_v,
    hf, rowf, q32, o32, tiles, hall, bbuf, usend, urecv,
    loc_sem, kv_sem, up_send, up_recv, down_send, down_recv, tile_send, tile_recv, b_sem, u_send, u_recv,
):
    g = lax.axis_index("group")
    t = lax.axis_index("tp")
    xy, zh, c = g // 4, (g // 2) % 2, g % 2
    z = zh * TP + t
    me = xy * 2 + c
    low, high = zh == 0, zh == 1

    def at_z(where):
        return (xy * 4 + (where // TP) * 2 + c, where % TP)

    def in_plane(i):
        p = (me + 1 + i) % PLANE
        return ((p // 2) * 4 + zh * 2 + p % 2, t)

    def remote(src, dst, send, recv, to):
        return pltpu.make_async_remote_copy(
            src_ref=src, dst_ref=dst, send_sem=send, recv_sem=recv, device_id=to, device_id_type=MESH
        )

    def wait_bytes(ref, sem):
        pltpu.make_async_copy(ref, ref, sem).wait()

    def times(start, stop, body):
        def step(i, _):
            body(i)
            return 0

        lax.fori_loop(start, stop, step, 0)

    small = [
        pltpu.make_async_copy(src, dst, loc_sem.at[i])
        for i, (src, dst) in enumerate(
            (
                (hidden_hbm, hidden_v),
                (down_hbm, down_v),
                (up_hbm, up_v),
                (queries_hbm, queries_v),
                (lengths_hbm, lengths_s),
                (gain_hbm, gain_v),
                (weight_hbm, weight_v),
            )
        )
    ]
    for copy in small[:6]:
        copy.start()

    barrier = pltpu.get_barrier_semaphore()

    def greet(to):
        pl.semaphore_signal(barrier, inc=1, device_id=to, device_id_type=MESH)

    @pl.when(z > 0)
    def _():
        greet(at_z(z - 1))

    @pl.when(z < 2 * TP - 1)
    def _():
        greet(at_z(z + 1))

    times(0, PLANE - 1, lambda i: greet(in_plane(i)))

    @pl.when(low)
    def _():
        times(t + 2, TP, lambda i: greet((g, i)))

    kv = []
    for r in range(ROWS):
        kv.append(
            (
                pltpu.make_async_copy(keys_hbm.at[r], keys_v.at[r], kv_sem.at[0, r]),
                pltpu.make_async_copy(values_hbm.at[r], values_v.at[r], kv_sem.at[1, r]),
            )
        )
        kv[r][0].start()
        kv[r][1].start()
    small[6].start()

    small[0].wait()
    for s in range(STEPS):
        hf[s * ROWS : (s + 1) * ROWS, :] = hidden_v[s].astype(F32)
    for k in range(KB):
        hall[z, k] = hf[:, k * HEAD : (k + 1) * HEAD].astype(BF)
    small[1].wait()
    small[2].wait()
    down = down_v[...].astype(F32)
    up = up_v[...].astype(F32)
    rowf[...] = jnp.zeros_like(rowf)
    for k in range(KB):
        rowf[k : k + 1, :] = down[:, k * HEAD : (k + 1) * HEAD]
    for k in range(2):
        rowf[KB + k : KB + k + 1, :] = up[:, k * HEAD : (k + 1) * HEAD]
    tiles[0, me] = rowf[0:8, :]
    hall[z, KB] = rowf[...].astype(BF)

    @pl.when(low)
    def _():
        pl.semaphore_wait(barrier, PLANE + t)

    @pl.when(high)
    def _():
        pl.semaphore_wait(barrier, PLANE + jnp.where(t < TP - 1, 1, 0))

    def up_copy(s):
        block = hall.at[(z - s + 2 * TP) % (2 * TP)]
        return remote(block, block, up_send.at[s], up_recv.at[s + 1], at_z((z + 1) % (2 * TP)))

    def down_copy(s):
        block = hall.at[(z + s) % (2 * TP), pl.ds(0, KB)]
        return remote(block, block, down_send.at[s], down_recv.at[s + 1], at_z((z + 2 * TP - 1) % (2 * TP)))

    def arrived_up(s):
        block = hall.at[(z - s + 2 * TP) % (2 * TP)]
        wait_bytes(block, up_recv.at[s])

    def arrived_down(s):
        block = hall.at[(z + s) % (2 * TP), pl.ds(0, KB)]
        wait_bytes(block, down_recv.at[s])

    sends_up = jnp.logical_or(low, t < TP - 1)
    sends_down = t > 0
    steps_up = jnp.where(low, t, TP)
    last_up = jnp.where(low, t + 1, jnp.where(t < TP - 1, TP, 0))
    steps_down = TP - 1 - t

    def tile_copy(which, i):
        return remote(
            tiles.at[which, me], tiles.at[which, me], tile_send.at[which], tile_recv.at[which], in_plane(i)
        )

    @pl.when(sends_up)
    def _():
        up_copy(0).start()

    times(0, PLANE - 1, lambda i: tile_copy(0, i).start())

    @pl.when(sends_down)
    def _():
        down_copy(0).start()

    def step_up(s):
        arrived_up(s)

        @pl.when(s < last_up)
        def _():
            up_copy(s).start()

    def step_down(s):
        arrived_down(s)

        @pl.when(sends_down)
        def _():
            down_copy(s).start()

    times(1, steps_up + 1, step_up)

    @pl.when(low)
    def _():
        times(1, steps_down + 1, step_down)

    def rows_of(which, k):
        return tiles[which, :, k, :].astype(BF)

    def factor_of(which):
        return jnp.concatenate(
            [jnp.concatenate([rows_of(which, k)] * 4, axis=0) for k in range(KB)], axis=1
        )

    def block_of(where):
        return jnp.concatenate([hall[where, k] for k in range(KB)], axis=1)

    def parts(block, a):
        u = dot_t(block, a)
        first = u.astype(BF).astype(F32)
        rest = u - first
        second = rest.astype(BF).astype(F32)
        third = (rest - second).astype(BF).astype(F32)
        lane = lax.broadcasted_iota(jnp.int32, u.shape, 1)
        zero = jnp.zeros_like(u)
        packed = jnp.where(lane < 32, first, jnp.where(lane < 64, second, jnp.where(lane < 96, third, zero)))
        return packed.astype(BF)

    def u_copy(src, which, where, send, to):
        return remote(src, urecv.at[which, where], u_send.at[send], u_recv.at[which], to)

    wait_bytes(tiles.at[0, pl.ds(0, PLANE - 1)], tile_recv.at[0])
    a_own = factor_of(0)

    @pl.when(high)
    def _():
        usend[...] = parts(block_of(t), a_own)
        times(0, TP, lambda i: u_copy(usend, 1, t, 1, (g - 2, i)).start())

    bbuf[0, :, 0:HEAD] = rows_of(0, KB)
    bbuf[0, :, HEAD : 2 * HEAD] = rows_of(0, KB + 1)

    def b_copy():
        return remote(bbuf.at[0], bbuf.at[1], b_sem.at[0], b_sem.at[1], at_z(z - TP))

    @pl.when(high)
    def _():
        b_copy().start()
        tiles[1, me] = hall[t, KB].astype(F32)[0:8]
        times(0, PLANE - 1, lambda i: tile_copy(1, i).start())

    urecv[0, t] = parts(block_of(z), a_own)

    def own_copy(which, send, i):
        return u_copy(urecv.at[which, t], which, t, send, (g, (t + 1 + i) % TP))

    @pl.when(low)
    def _():
        times(0, TP - 1, lambda i: own_copy(0, 0, i).start())

    small[3].wait()
    for s in range(STEPS):
        for h in range(HEADS):
            q32[pl.ds(s * HEADS + h, ROWS, stride=QUERIES), :] = queries_v[
                s, :, h * HEAD : (h + 1) * HEAD
            ].astype(F32)
    small[4].wait()
    factor = HEAD ** (-0.5)

    def cached(r):
        kv[r][0].wait()
        q = q32[r * QUERIES : (r + 1) * QUERIES, :].astype(BF)
        scores = dot_t(q, keys_v[r]) * factor
        slot = lax.broadcasted_iota(jnp.int32, scores.shape, 1)
        scores = jnp.where(slot < lengths_s[r], scores, -jnp.inf)
        top = jnp.max(scores, axis=1, keepdims=True)
        p = jnp.exp(scores - top)
        total = jnp.sum(p, axis=1, keepdims=True)
        kv[r][1].wait()
        return top, total, dot(p.astype(BF), values_v[r])

    rows = [cached(r) for r in range(ROWS)]
    top_c = jnp.concatenate([r[0] for r in rows], axis=0)
    total_c = jnp.concatenate([r[1] for r in rows], axis=0)
    acc_c = jnp.concatenate([r[2] for r in rows], axis=0)

    @pl.when(high)
    def _():
        times(1, steps_down + 1, step_down)
        times(0, TP - 1, lambda i: own_copy(0, 0, i).start())
        wait_bytes(tiles.at[1, pl.ds(0, PLANE - 1)], tile_recv.at[1])
        urecv[1, t] = parts(block_of(z), factor_of(1))
        times(0, TP - 1, lambda i: own_copy(1, 2, i).start())
        bbuf[1, :, 0:HEAD] = rows_of(1, KB)
        bbuf[1, :, HEAD : 2 * HEAD] = rows_of(1, KB + 1)

    small[6].wait()
    base = jnp.zeros((TOKENS, 2 * HEAD), F32)
    for i in range(TP):
        base = base + dot(block_of(zh * TP + i), weight_v[i * KB * HEAD : (i + 1) * KB * HEAD, :])
    small[5].wait()
    gain = gain_v[...].reshape(1, HEAD)

    def update(which):
        b = jnp.concatenate([bbuf[which]] * 4, axis=0)
        return dot(urecv[which].reshape(TP * TOKENS, HEAD), b)

    def fold(x):
        return ADAPTER_SCALE * jnp.sum(x.reshape(TP, TOKENS, 2 * HEAD), axis=0)

    wait_bytes(urecv.at[0, pl.ds(0, TP - 1)], u_recv.at[0])
    base = base + fold(update(0))

    @pl.when(low)
    def _():
        wait_bytes(urecv.at[1], u_recv.at[1])
        wait_bytes(bbuf.at[1], b_sem.at[1])

    @pl.when(high)
    def _():
        wait_bytes(urecv.at[1, pl.ds(0, TP - 1)], u_recv.at[1])

    projected = base + fold(update(1))

    raw = projected[:, 0:HEAD]
    value = projected[:, HEAD : 2 * HEAD]
    scale = lax.rsqrt(jnp.mean(raw * raw, axis=1, keepdims=True) + NORM_EPS)
    key = raw * scale * gain
    for s in range(STEPS):
        ent_ref[s, :, 0:HEAD] = key[s * ROWS : (s + 1) * ROWS].astype(BF)
        ent_ref[s, :, HEAD : 2 * HEAD] = value[s * ROWS : (s + 1) * ROWS].astype(BF)

    scores = dot_t(q32[...].astype(BF), key.astype(BF)) * factor
    qi = lax.broadcasted_iota(jnp.int32, scores.shape, 0)
    ki = lax.broadcasted_iota(jnp.int32, scores.shape, 1)
    seen = (ki % ROWS == qi // QUERIES) & (ki // ROWS <= (qi % QUERIES) // HEADS)
    scores = jnp.where(seen, scores, -jnp.inf)
    top = jnp.maximum(top_c, jnp.max(scores, axis=1, keepdims=True))
    p = jnp.exp(scores - top)
    carry = jnp.exp(top_c - top)
    total = carry * total_c + jnp.sum(p, axis=1, keepdims=True)
    o32[...] = (carry * acc_c + dot(p.astype(BF), value.astype(BF))) / total
    for s in range(STEPS):
        for h in range(HEADS):
            att_ref[s, :, h * HEAD : (h + 1) * HEAD] = o32[
                pl.ds(s * HEADS + h, ROWS, stride=QUERIES), :
            ].astype(BF)

    times(0, last_up, lambda s: up_copy(s).wait_send())

    @pl.when(sends_down)
    def _():
        times(0, steps_down + 1, lambda s: down_copy(s).wait_send())

    wait_bytes(tiles.at[0, pl.ds(0, PLANE - 1)], tile_send.at[0])
    wait_bytes(urecv.at[0, pl.ds(0, TP - 1)], u_send.at[0])

    @pl.when(high)
    def _():
        wait_bytes(tiles.at[1, pl.ds(0, PLANE - 1)], tile_send.at[1])
        wait_bytes(urecv.at[1], u_send.at[1])
        wait_bytes(urecv.at[1, pl.ds(0, TP - 1)], u_send.at[2])
        b_copy().wait_send()


def per_device(hidden, queries, keys, values, lengths, weight, down, up, gain):
    dma = pltpu.SemaphoreType.DMA
    return pl.pallas_call(
        kernel,
        name="decode",
        out_shape=(
            pltpu.VMEM(queries.shape, BF),
            pltpu.VMEM((STEPS, ROWS, 2 * HEAD), BF),
        ),
        in_specs=[pl.BlockSpec(memory_space=pltpu.HBM)] * 9,
        out_specs=(pl.BlockSpec(memory_space=pltpu.VMEM),) * 2,
        scratch_shapes=[
            pltpu.VMEM(hidden.shape, BF),
            pltpu.VMEM(queries.shape, BF),
            pltpu.VMEM(keys.shape, BF),
            pltpu.VMEM(values.shape, BF),
            pltpu.SMEM(lengths.shape, jnp.int32),
            pltpu.VMEM(weight.shape, BF),
            pltpu.VMEM(down.shape, BF),
            pltpu.VMEM(up.shape, BF),
            pltpu.VMEM(gain.shape, F32),
            pltpu.VMEM((TOKENS, KB * HEAD), F32),
            pltpu.VMEM((TOKENS, HEAD), F32),
            pltpu.VMEM((ROWS * QUERIES, HEAD), F32),
            pltpu.VMEM((ROWS * QUERIES, HEAD), F32),
            pltpu.VMEM((2, PLANE, 8, HEAD), F32),
            pltpu.VMEM((2 * TP, KB + 1, TOKENS, HEAD), BF),
            pltpu.VMEM((2, PLANE, 2 * HEAD), BF),
            pltpu.VMEM((TOKENS, HEAD), BF),
            pltpu.VMEM((2, TP, TOKENS, HEAD), BF),
            dma((7,)),
            dma((2, ROWS)),
            dma((TP + 1,)),
            dma((TP + 1,)),
            dma((TP + 1,)),
            dma((TP + 1,)),
            dma((2,)),
            dma((2,)),
            dma((2,)),
            dma((3,)),
            dma((2,)),
        ],
        compiler_params=pltpu.CompilerParams(
            collective_id=0, has_side_effects=True, vmem_limit_bytes=60 * 1024 * 1024
        ),
    )(hidden, queries, keys, values, lengths, weight, down, up, gain)


def solution(mesh):
    return jax.shard_map(
        per_device,
        mesh=mesh,
        in_specs=(
            P(None, "group", "tp"),
            P(None, "group", "tp"),
            P("group", None, "tp"),
            P("group", None, "tp"),
            P("group"),
            P(None, "tp"),
            P("group", "tp"),
            P("group", "tp"),
            P(),
        ),
        out_specs=(P(None, "group", "tp"), P(None, "group", "tp")),
        check_vma=False,
    )
```

time: 41.2 us -> 59.6 us (1.45)
  the two profiles are of different devices: /device:TPU:1 before, /device:TPU:480 now
where the time goes in v3:
time: 59.6 us; the launch traced here: 59.5 us
  Pallas kernels  57.7 us (97%)
  local copies, waits for them, and re-layouts  1.22 us (2%)
  between operations  0.64 us (1%)
    pallas_call x1, Pallas kernels, per_device(): pl.pallas_call(kernel, name='decode', out_shape=(pltpu.VMEM(queries.shape...  57.7 us
    unnamed x2, local copies, waits for them, and re-layouts  1.22 us

profile of v3, /device:TPU:480, one launch (start us, length us, event | category | flops | bytes accessed | tf_op | source)
XLA Modules:
  0.0 59.5 jit_solution(11815468818127266632)
XLA Ops:
  0.6 57.7 %decode.1 = (bf16[4,4,1024]{2,1,0:T(4,128)(2,1)S(1)}, bf16[4,4,256]{2,1,0:T(4,128)(2,1)S(1)}) custom-call(bf16[4,4,640]{2,1,0:T(4,128)(2,1)} %hidden_hbm.1, bf16[4,4,1024]{2,1,0:T(4,128)(2,1)} %queries_hbm.1, bf16[4,1024,128]{2,1,0:T(8,128)(2,1)} %keys_hbm.1, bf16[4,1024,128]{2,1,0:T(8,128)(2,1)} %values_hbm.1, s32[4]{0:T(128)} %lengths_hbm.1, ...), custom_call_target="tpu_custom_call" | custom-call | tf_op jit(solution)/shard_map/decode/pallas_call | solution.py:360
  58.3 0.6 %copy.13 = bf16[4,4,1024]{2,1,0:T(4,128)(2,1)} copy(bf16[4,4,1024]{2,1,0:T(4,128)(2,1)S(1)} %get-tuple-element.2) | data formatting | bytes 65536
  58.9 0.6 %copy.14 = bf16[4,4,256]{2,1,0:T(4,128)(2,1)} copy(bf16[4,4,256]{2,1,0:T(4,128)(2,1)S(1)} %get-tuple-element.3) | data formatting | bytes 16384

commit v4 on v3

--- a/solution.py
+++ b/solution.py
@@ -12,6 +12,7 @@
 TOKENS = STEPS * ROWS
 QUERIES = STEPS * HEADS
 TP = 8
+QUAD = 4
 PLANE = 32
 KB = 5
 
@@ -35,7 +36,7 @@
     att_ref, ent_ref,
     hidden_v, queries_v, keys_v, values_v, lengths_s, weight_v, down_v, up_v, gain_v,
     hf, rowf, q32, o32, tiles, hall, bbuf, usend, urecv,
-    loc_sem, kv_sem, up_send, up_recv, down_send, down_recv, tile_send, tile_recv, b_sem, u_send, u_recv,
+    loc_sem, kv_sem, block_send, block_recv, quad_send, quad_recv, tile_send, tile_recv, b_sem, u_send, u_recv,
 ):
     g = lax.axis_index("group")
     t = lax.axis_index("tp")
@@ -48,7 +49,7 @@
         return (xy * 4 + (where // TP) * 2 + c, where % TP)
 
     def in_plane(i):
-        p = (me + 1 + i) % PLANE
+        p = jnp.where(i < me, i, i + 1)
         return ((p // 2) * 4 + zh * 2 + p % 2, t)
 
     def remote(src, dst, send, recv, to):
@@ -88,19 +89,15 @@
     def greet(to):
         pl.semaphore_signal(barrier, inc=1, device_id=to, device_id_type=MESH)
 
-    @pl.when(z > 0)
-    def _():
-        greet(at_z(z - 1))
-
-    @pl.when(z < 2 * TP - 1)
-    def _():
-        greet(at_z(z + 1))
-
+    def greet_z(d):
+        greet(at_z((z - d + 2 * TP) % (2 * TP)))
+
+        @pl.when(z + d < 2 * TP)
+        def _():
+            greet(at_z(z + d))
+
+    times(1, QUAD + 1, greet_z)
     times(0, PLANE - 1, lambda i: greet(in_plane(i)))
-
-    @pl.when(low)
-    def _():
-        times(t + 2, TP, lambda i: greet((g, i)))
 
     kv = []
     for r in range(ROWS):
@@ -133,68 +130,83 @@
 
     @pl.when(low)
     def _():
-        pl.semaphore_wait(barrier, PLANE + t)
-
-    @pl.when(high)
-    def _():
-        pl.semaphore_wait(barrier, PLANE + jnp.where(t < TP - 1, 1, 0))
-
-    def up_copy(s):
-        block = hall.at[(z - s + 2 * TP) % (2 * TP)]
-        return remote(block, block, up_send.at[s], up_recv.at[s + 1], at_z((z + 1) % (2 * TP)))
-
-    def down_copy(s):
-        block = hall.at[(z + s) % (2 * TP), pl.ds(0, KB)]
-        return remote(block, block, down_send.at[s], down_recv.at[s + 1], at_z((z + 2 * TP - 1) % (2 * TP)))
-
-    def arrived_up(s):
-        block = hall.at[(z - s + 2 * TP) % (2 * TP)]
-        wait_bytes(block, up_recv.at[s])
-
-    def arrived_down(s):
-        block = hall.at[(z + s) % (2 * TP), pl.ds(0, KB)]
-        wait_bytes(block, down_recv.at[s])
-
-    sends_up = jnp.logical_or(low, t < TP - 1)
-    sends_down = t > 0
-    steps_up = jnp.where(low, t, TP)
-    last_up = jnp.where(low, t + 1, jnp.where(t < TP - 1, TP, 0))
-    steps_down = TP - 1 - t
+        pl.semaphore_wait(barrier, PLANE - 1 + QUAD + jnp.minimum(t, QUAD))
+
+    @pl.when(high)
+    def _():
+        pl.semaphore_wait(barrier, PLANE - 1 + 2 * QUAD)
+
+    first_quad = t < QUAD
+    above, below = (z + QUAD) % (2 * TP), (z + 2 * TP - QUAD) % (2 * TP)
+    sends_up = jnp.logical_or(low, first_quad)
+    sends_down = jnp.logical_not(first_quad)
+    passes_on = low != first_quad
+
+    def up_copy():
+        return remote(hall.at[z], hall.at[z], block_send.at[0], block_recv.at[0], at_z(above))
+
+    def down_copy():
+        block = hall.at[z, pl.ds(0, KB)]
+        return remote(block, block, block_send.at[1], block_recv.at[1], at_z(below))
+
+    def pass_copy():
+        return remote(hall.at[below], hall.at[below], block_send.at[2], block_recv.at[2], at_z(above))
+
+    def from_below():
+        wait_bytes(hall.at[below], block_recv.at[0])
+
+    def from_above():
+        wait_bytes(hall.at[above, pl.ds(0, KB)], block_recv.at[1])
+
+    apart = jnp.where(first_quad, QUAD, -QUAD)
+    corner = z - t % QUAD
+
+    def quad_copy(which, j):
+        where = z + which * apart
+        block = hall.at[where, pl.ds(0, KB)]
+        to = corner + (t + 1 + j) % QUAD
+        return remote(block, block, quad_send.at[which, j], quad_recv.at[which, j], at_z(to))
+
+    def quad_arrived(which, j):
+        where = corner + (t + 2 * QUAD - 1 - j) % QUAD + which * apart
+        wait_bytes(hall.at[where, pl.ds(0, KB)], quad_recv.at[which, j])
 
     def tile_copy(which, i):
         return remote(
             tiles.at[which, me], tiles.at[which, me], tile_send.at[which], tile_recv.at[which], in_plane(i)
         )
 
-    @pl.when(sends_up)
-    def _():
-        up_copy(0).start()
+    def send_down():
+        @pl.when(sends_down)
+        def _():
+            down_copy().start()
+
+    @pl.when(low)
+    def _():
+        up_copy().start()
+        send_down()
 
     times(0, PLANE - 1, lambda i: tile_copy(0, i).start())
 
-    @pl.when(sends_down)
-    def _():
-        down_copy(0).start()
-
-    def step_up(s):
-        arrived_up(s)
-
-        @pl.when(s < last_up)
-        def _():
-            up_copy(s).start()
-
-    def step_down(s):
-        arrived_down(s)
-
-        @pl.when(sends_down)
-        def _():
-            down_copy(s).start()
-
-    times(1, steps_up + 1, step_up)
-
     @pl.when(low)
     def _():
-        times(1, steps_down + 1, step_down)
+        times(0, QUAD - 1, lambda j: quad_copy(0, j).start())
+
+        @pl.when(first_quad)
+        def _():
+            from_above()
+
+        @pl.when(jnp.logical_not(first_quad))
+        def _():
+            from_below()
+            pass_copy().start()
+
+        times(0, QUAD - 1, lambda j: quad_copy(1, j).start())
+
+    @pl.when(jnp.logical_and(high, first_quad))
+    def _():
+        from_below()
+        pass_copy().start()
 
     def rows_of(which, k):
         return tiles[which, :, k, :].astype(BF)
@@ -226,6 +238,7 @@
 
     @pl.when(high)
     def _():
+        wait_bytes(hall.at[t], block_recv.at[2])
         usend[...] = parts(block_of(t), a_own)
         times(0, TP, lambda i: u_copy(usend, 1, t, 1, (g - 2, i)).start())
 
@@ -240,6 +253,13 @@
         b_copy().start()
         tiles[1, me] = hall[t, KB].astype(F32)[0:8]
         times(0, PLANE - 1, lambda i: tile_copy(1, i).start())
+
+        @pl.when(first_quad)
+        def _():
+            up_copy().start()
+
+        send_down()
+        times(0, QUAD - 1, lambda j: quad_copy(0, j).start())
 
     urecv[0, t] = parts(block_of(z), a_own)
 
@@ -278,7 +298,15 @@
 
     @pl.when(high)
     def _():
-        times(1, steps_down + 1, step_down)
+        @pl.when(first_quad)
+        def _():
+            from_above()
+
+        @pl.when(jnp.logical_not(first_quad))
+        def _():
+            from_below()
+
+        times(0, QUAD - 1, lambda j: quad_copy(1, j).start())
         times(0, TP - 1, lambda i: own_copy(0, 0, i).start())
         wait_bytes(tiles.at[1, pl.ds(0, PLANE - 1)], tile_recv.at[1])
         urecv[1, t] = parts(block_of(z), factor_of(1))
@@ -286,6 +314,8 @@
         bbuf[1, :, 0:HEAD] = rows_of(1, KB)
         bbuf[1, :, HEAD : 2 * HEAD] = rows_of(1, KB + 1)
 
+    for which in range(2):
+        times(0, QUAD - 1, lambda j, which=which: quad_arrived(which, j))
     small[6].wait()
     base = jnp.zeros((TOKENS, 2 * HEAD), F32)
     for i in range(TP):
@@ -338,12 +368,20 @@
                 pl.ds(s * HEADS + h, ROWS, stride=QUERIES), :
             ].astype(BF)
 
-    times(0, last_up, lambda s: up_copy(s).wait_send())
+    @pl.when(sends_up)
+    def _():
+        up_copy().wait_send()
 
     @pl.when(sends_down)
     def _():
-        times(0, steps_down + 1, lambda s: down_copy(s).wait_send())
-
+        down_copy().wait_send()
+
+    @pl.when(passes_on)
+    def _():
+        pass_copy().wait_send()
+
+    for which in range(2):
+        times(0, QUAD - 1, lambda j, which=which: quad_copy(which, j).wait_send())
     wait_bytes(tiles.at[0, pl.ds(0, PLANE - 1)], tile_send.at[0])
     wait_bytes(urecv.at[0, pl.ds(0, TP - 1)], u_send.at[0])
 
@@ -387,10 +425,10 @@
             pltpu.VMEM((2, TP, TOKENS, HEAD), BF),
             dma((7,)),
             dma((2, ROWS)),
-            dma((TP + 1,)),
-            dma((TP + 1,)),
-            dma((TP + 1,)),
-            dma((TP + 1,)),
+            dma((3,)),
+            dma((3,)),
+            dma((2, QUAD - 1)),
+            dma((2, QUAD - 1)),
             dma((2,)),
             dma((2,)),
             dma((2,)),

time: 59.6 us -> 33.4 us (0.56)
  the two profiles are of different devices: /device:TPU:480 before, /device:TPU:62 now
where the time goes in v4:
time: 33.4 us; the launch traced here: 33.3 us
  Pallas kernels  31.4 us (94%)
  local copies, waits for them, and re-layouts  1.22 us (4%)
  between operations  0.64 us (2%)
    pallas_call x1, Pallas kernels, per_device(): pl.pallas_call(kernel, name='decode', out_shape=(pltpu.VMEM(queries.shape...  31.4 us
    unnamed x2, local copies, waits for them, and re-layouts  1.22 us

profile of v4, /device:TPU:62, one launch (start us, length us, event | category | flops | bytes accessed | tf_op | source)
XLA Modules:
  0.0 33.3 jit_solution(1611486124114556579)
XLA Ops:
  0.6 31.4 %decode.1 = (bf16[4,4,1024]{2,1,0:T(4,128)(2,1)S(1)}, bf16[4,4,256]{2,1,0:T(4,128)(2,1)S(1)}) custom-call(bf16[4,4,640]{2,1,0:T(4,128)(2,1)} %hidden_hbm.1, bf16[4,4,1024]{2,1,0:T(4,128)(2,1)} %queries_hbm.1, bf16[4,1024,128]{2,1,0:T(8,128)(2,1)} %keys_hbm.1, bf16[4,1024,128]{2,1,0:T(8,128)(2,1)} %values_hbm.1, s32[4]{0:T(128)} %lengths_hbm.1, ...), custom_call_target="tpu_custom_call" | custom-call | tf_op jit(solution)/shard_map/decode/pallas_call | solution.py:398
  32.0 0.6 %copy.13 = bf16[4,4,1024]{2,1,0:T(4,128)(2,1)} copy(bf16[4,4,1024]{2,1,0:T(4,128)(2,1)S(1)} %get-tuple-element.2) | data formatting | bytes 65536
  32.7 0.6 %copy.14 = bf16[4,4,256]{2,1,0:T(4,128)(2,1)} copy(bf16[4,4,256]{2,1,0:T(4,128)(2,1)S(1)} %get-tuple-element.3) | data formatting | bytes 16384

commit v5 on v4

--- a/solution.py
+++ b/solution.py
@@ -33,10 +33,10 @@
 
 def kernel(
     hidden_hbm, queries_hbm, keys_hbm, values_hbm, lengths_hbm, weight_hbm, down_hbm, up_hbm, gain_hbm,
-    att_ref, ent_ref,
+    o32, e32,
     hidden_v, queries_v, keys_v, values_v, lengths_s, weight_v, down_v, up_v, gain_v,
-    hf, rowf, q32, o32, tiles, hall, bbuf, usend, urecv,
-    loc_sem, kv_sem, block_send, block_recv, quad_send, quad_recv, tile_send, tile_recv, b_sem, u_send, u_recv,
+    hf, rowf, q32, tiles, hall, wrap, bbuf, usend, urecv,
+    loc_sem, kv_sem, block_send, block_recv, quad_send, quad_recv, tile_send, tile_recv, b_sem, wrap_send, wrap_recv, u_send, u_recv,
 ):
     g = lax.axis_index("group")
     t = lax.axis_index("tp")
@@ -44,6 +44,7 @@
     z = zh * TP + t
     me = xy * 2 + c
     low, high = zh == 0, zh == 1
+    round_about = t >= TP - 2
 
     def at_z(where):
         return (xy * 4 + (where // TP) * 2 + c, where % TP)
@@ -97,6 +98,20 @@
             greet(at_z(z + d))
 
     times(1, QUAD + 1, greet_z)
+
+    @pl.when(low)
+    def _():
+        greet(at_z(z + TP))
+
+    @pl.when(z == 0)
+    def _():
+        greet(at_z(TP - 2))
+        greet(at_z(TP - 1))
+
+    @pl.when(z >= 2 * TP - 2)
+    def _():
+        greet(at_z(0))
+
     times(0, PLANE - 1, lambda i: greet(in_plane(i)))
 
     kv = []
@@ -130,17 +145,19 @@
 
     @pl.when(low)
     def _():
-        pl.semaphore_wait(barrier, PLANE - 1 + QUAD + jnp.minimum(t, QUAD))
-
-    @pl.when(high)
-    def _():
-        pl.semaphore_wait(barrier, PLANE - 1 + 2 * QUAD)
+        extra = jnp.where(t == 0, 2, jnp.where(round_about, 1, 0))
+        pl.semaphore_wait(barrier, PLANE - 1 + QUAD + jnp.minimum(t, QUAD) + extra)
+
+    @pl.when(high)
+    def _():
+        pl.semaphore_wait(barrier, PLANE + 2 * QUAD)
 
     first_quad = t < QUAD
     above, below = (z + QUAD) % (2 * TP), (z + 2 * TP - QUAD) % (2 * TP)
-    sends_up = jnp.logical_or(low, first_quad)
+    sends_up = jnp.logical_or(jnp.logical_and(low, jnp.logical_not(round_about)), jnp.logical_and(high, first_quad))
     sends_down = jnp.logical_not(first_quad)
-    passes_on = low != first_quad
+    passes_low = jnp.logical_and(low, sends_down)
+    passes_high = jnp.logical_and(high, t < TP - 2 - QUAD)
 
     def up_copy():
         return remote(hall.at[z], hall.at[z], block_send.at[0], block_recv.at[0], at_z(above))
@@ -151,6 +168,12 @@
 
     def pass_copy():
         return remote(hall.at[below], hall.at[below], block_send.at[2], block_recv.at[2], at_z(above))
+
+    def round_copy():
+        return remote(hall.at[z], wrap.at[t - (TP - 2)], wrap_send.at[0], wrap_recv.at[t - (TP - 2)], at_z(0))
+
+    def wrap_copy(i):
+        return remote(wrap.at[i], hall.at[TP - 2 + i], wrap_send.at[i], block_recv.at[2], at_z(2 * TP - 2 + i))
 
     def from_below():
         wait_bytes(hall.at[below], block_recv.at[0])
@@ -181,9 +204,19 @@
         def _():
             down_copy().start()
 
+    def b_copy():
+        return remote(bbuf.at[0], bbuf.at[1], b_sem.at[0], b_sem.at[1], at_z(z - TP))
+
     @pl.when(low)
     def _():
-        up_copy().start()
+        @pl.when(round_about)
+        def _():
+            round_copy().start()
+
+        @pl.when(jnp.logical_not(round_about))
+        def _():
+            up_copy().start()
+
         send_down()
 
     times(0, PLANE - 1, lambda i: tile_copy(0, i).start())
@@ -203,10 +236,24 @@
 
         times(0, QUAD - 1, lambda j: quad_copy(1, j).start())
 
-    @pl.when(jnp.logical_and(high, first_quad))
+    @pl.when(high)
+    def _():
+        send_down()
+
+    @pl.when(passes_high)
     def _():
         from_below()
         pass_copy().start()
+
+    @pl.when(jnp.logical_and(high, first_quad))
+    def _():
+        up_copy().start()
+
+    @pl.when(z == 0)
+    def _():
+        for i in (0, 1):
+            wait_bytes(wrap.at[i], wrap_recv.at[i])
+            wrap_copy(i).start()
 
     def rows_of(which, k):
         return tiles[which, :, k, :].astype(BF)
@@ -236,29 +283,21 @@
     wait_bytes(tiles.at[0, pl.ds(0, PLANE - 1)], tile_recv.at[0])
     a_own = factor_of(0)
 
-    @pl.when(high)
-    def _():
+    for k in range(2):
+        bbuf[0, :, k * HEAD : (k + 1) * HEAD] = rows_of(0, KB + k)
+
+    @pl.when(high)
+    def _():
+        b_copy().start()
         wait_bytes(hall.at[t], block_recv.at[2])
         usend[...] = parts(block_of(t), a_own)
         times(0, TP, lambda i: u_copy(usend, 1, t, 1, (g - 2, i)).start())
 
-    bbuf[0, :, 0:HEAD] = rows_of(0, KB)
-    bbuf[0, :, HEAD : 2 * HEAD] = rows_of(0, KB + 1)
-
-    def b_copy():
-        return remote(bbuf.at[0], bbuf.at[1], b_sem.at[0], b_sem.at[1], at_z(z - TP))
-
-    @pl.when(high)
-    def _():
-        b_copy().start()
+    @pl.when(high)
+    def _():
         tiles[1, me] = hall[t, KB].astype(F32)[0:8]
         times(0, PLANE - 1, lambda i: tile_copy(1, i).start())
 
-        @pl.when(first_quad)
-        def _():
-            up_copy().start()
-
-        send_down()
         times(0, QUAD - 1, lambda j: quad_copy(0, j).start())
 
     urecv[0, t] = parts(block_of(z), a_own)
@@ -311,8 +350,8 @@
         wait_bytes(tiles.at[1, pl.ds(0, PLANE - 1)], tile_recv.at[1])
         urecv[1, t] = parts(block_of(z), factor_of(1))
         times(0, TP - 1, lambda i: own_copy(1, 2, i).start())
-        bbuf[1, :, 0:HEAD] = rows_of(1, KB)
-        bbuf[1, :, HEAD : 2 * HEAD] = rows_of(1, KB + 1)
+        for k in range(2):
+            bbuf[1, :, k * HEAD : (k + 1) * HEAD] = rows_of(1, KB + k)
 
     for which in range(2):
         times(0, QUAD - 1, lambda j, which=which: quad_arrived(which, j))
@@ -335,8 +374,8 @@
 
     @pl.when(low)
     def _():
+        wait_bytes(bbuf.at[1], b_sem.at[1])
         wait_bytes(urecv.at[1], u_recv.at[1])
-        wait_bytes(bbuf.at[1], b_sem.at[1])
 
     @pl.when(high)
     def _():
@@ -348,9 +387,8 @@
     value = projected[:, HEAD : 2 * HEAD]
     scale = lax.rsqrt(jnp.mean(raw * raw, axis=1, keepdims=True) + NORM_EPS)
     key = raw * scale * gain
-    for s in range(STEPS):
-        ent_ref[s, :, 0:HEAD] = key[s * ROWS : (s + 1) * ROWS].astype(BF)
-        ent_ref[s, :, HEAD : 2 * HEAD] = value[s * ROWS : (s + 1) * ROWS].astype(BF)
+    e32[:, 0:HEAD] = key
+    e32[:, HEAD : 2 * HEAD] = value
 
     scores = dot_t(q32[...].astype(BF), key.astype(BF)) * factor
     qi = lax.broadcasted_iota(jnp.int32, scores.shape, 0)
@@ -362,45 +400,57 @@
     carry = jnp.exp(top_c - top)
     total = carry * total_c + jnp.sum(p, axis=1, keepdims=True)
     o32[...] = (carry * acc_c + dot(p.astype(BF), value.astype(BF))) / total
+    @pl.when(sends_up)
+    def _():
+        up_copy().wait_send()
+
+    @pl.when(sends_down)
+    def _():
+        down_copy().wait_send()
+
+    @pl.when(jnp.logical_or(passes_low, passes_high))
+    def _():
+        pass_copy().wait_send()
+
+    @pl.when(jnp.logical_and(low, round_about))
+    def _():
+        round_copy().wait_send()
+
+    @pl.when(z == 0)
+    def _():
+        wrap_copy(0).wait_send()
+        wrap_copy(1).wait_send()
+
+    for which in range(2):
+        times(0, QUAD - 1, lambda j, which=which: quad_copy(which, j).wait_send())
+    wait_bytes(tiles.at[0, pl.ds(0, PLANE - 1)], tile_send.at[0])
+    wait_bytes(urecv.at[0, pl.ds(0, TP - 1)], u_send.at[0])
+
+    @pl.when(high)
+    def _():
+        wait_bytes(urecv.at[1], u_send.at[1])
+        wait_bytes(urecv.at[1, pl.ds(0, TP - 1)], u_send.at[2])
+        b_copy().wait_send()
+        wait_bytes(tiles.at[1, pl.ds(0, PLANE - 1)], tile_send.at[1])
+
+
+def write_out(o32, e32, att_ref, ent_ref):
     for s in range(STEPS):
+        ent_ref[s] = e32[s * ROWS : (s + 1) * ROWS, :].astype(BF)
         for h in range(HEADS):
             att_ref[s, :, h * HEAD : (h + 1) * HEAD] = o32[
                 pl.ds(s * HEADS + h, ROWS, stride=QUERIES), :
             ].astype(BF)
 
-    @pl.when(sends_up)
-    def _():
-        up_copy().wait_send()
-
-    @pl.when(sends_down)
-    def _():
-        down_copy().wait_send()
-
-    @pl.when(passes_on)
-    def _():
-        pass_copy().wait_send()
-
-    for which in range(2):
-        times(0, QUAD - 1, lambda j, which=which: quad_copy(which, j).wait_send())
-    wait_bytes(tiles.at[0, pl.ds(0, PLANE - 1)], tile_send.at[0])
-    wait_bytes(urecv.at[0, pl.ds(0, TP - 1)], u_send.at[0])
-
-    @pl.when(high)
-    def _():
-        wait_bytes(tiles.at[1, pl.ds(0, PLANE - 1)], tile_send.at[1])
-        wait_bytes(urecv.at[1], u_send.at[1])
-        wait_bytes(urecv.at[1, pl.ds(0, TP - 1)], u_send.at[2])
-        b_copy().wait_send()
-
 
 def per_device(hidden, queries, keys, values, lengths, weight, down, up, gain):
     dma = pltpu.SemaphoreType.DMA
-    return pl.pallas_call(
+    attention, entries = pl.pallas_call(
         kernel,
         name="decode",
         out_shape=(
-            pltpu.VMEM(queries.shape, BF),
-            pltpu.VMEM((STEPS, ROWS, 2 * HEAD), BF),
+            pltpu.VMEM((ROWS * QUERIES, HEAD), F32),
+            pltpu.VMEM((TOKENS, 2 * HEAD), F32),
         ),
         in_specs=[pl.BlockSpec(memory_space=pltpu.HBM)] * 9,
         out_specs=(pl.BlockSpec(memory_space=pltpu.VMEM),) * 2,
@@ -417,9 +467,9 @@
             pltpu.VMEM((TOKENS, KB * HEAD), F32),
             pltpu.VMEM((TOKENS, HEAD), F32),
             pltpu.VMEM((ROWS * QUERIES, HEAD), F32),
-            pltpu.VMEM((ROWS * QUERIES, HEAD), F32),
             pltpu.VMEM((2, PLANE, 8, HEAD), F32),
             pltpu.VMEM((2 * TP, KB + 1, TOKENS, HEAD), BF),
+            pltpu.VMEM((2, KB + 1, TOKENS, HEAD), BF),
             pltpu.VMEM((2, PLANE, 2 * HEAD), BF),
             pltpu.VMEM((TOKENS, HEAD), BF),
             pltpu.VMEM((2, TP, TOKENS, HEAD), BF),
@@ -432,6 +482,8 @@
             dma((2,)),
             dma((2,)),
             dma((2,)),
+            dma((2,)),
+            dma((2,)),
             dma((3,)),
             dma((2,)),
         ],
@@ -439,6 +491,17 @@
             collective_id=0, has_side_effects=True, vmem_limit_bytes=60 * 1024 * 1024
         ),
     )(hidden, queries, keys, values, lengths, weight, down, up, gain)
+    return pl.pallas_call(
+        write_out,
+        name="write_out",
+        out_shape=(
+            jax.ShapeDtypeStruct(queries.shape, BF),
+            jax.ShapeDtypeStruct((STEPS, ROWS, 2 * HEAD), BF),
+        ),
+        in_specs=[pl.BlockSpec(memory_space=pltpu.VMEM)] * 2,
+        out_specs=(pl.BlockSpec(memory_space=pltpu.VMEM),) * 2,
+        compiler_params=pltpu.CompilerParams(vmem_limit_bytes=2 * 1024 * 1024),
+    )(attention, entries)
 
 
 def solution(mesh):

time: 33.4 us -> 31.8 us (0.952)
  the two profiles are of different devices: /device:TPU:62 before, /device:TPU:48 now
where the time goes in v5:
time: 31.8 us; the launch traced here: 31.7 us
  Pallas kernels  31.1 us (98%)
  between operations  0.64 us (2%)
    pallas_call x1, Pallas kernels, per_device(): pl.pallas_call(kernel, name='decode', out_shape=(pltpu.VMEM((ROWS * QUERI...  30.4 us
    pallas_call x1, Pallas kernels, per_device(): pl.pallas_call(write_out, name='write_out', out_shape=(jax.ShapeDtypeStru...  0.67 us

profile of v5, /device:TPU:48, one launch (start us, length us, event | category | flops | bytes accessed | tf_op | source)
XLA Modules:
  0.0 31.7 jit_solution(18250400924478293823)
XLA Ops:
  0.6 30.4 %decode.1 = (f32[128,128]{1,0:T(8,128)S(1)}, f32[16,256]{1,0:T(8,128)S(1)}) custom-call(bf16[4,4,640]{2,1,0:T(4,128)(2,1)} %hidden_hbm.1, bf16[4,4,1024]{2,1,0:T(4,128)(2,1)} %queries_hbm.1, bf16[4,1024,128]{2,1,0:T(8,128)(2,1)} %keys_hbm.1, bf16[4,1024,128]{2,1,0:T(8,128)(2,1)} %values_hbm.1, s32[4]{0:T(128)} %lengths_hbm.1, bf16[5120,256]{1,0:T(8,128)(2,1)} %weight_hbm.1, ...), custom_call_target="tpu_custom_call" | custom-call | tf_op jit(solution)/shard_map/decode/pallas_call | solution.py:448
  31.0 0.7 %write_out.1 = (bf16[4,4,1024]{2,1,0:T(4,128)(2,1)}, bf16[4,4,256]{2,1,0:T(4,128)(2,1)}) custom-call(f32[128,128]{1,0:T(8,128)S(1)} %get-tuple-element.4.o32, f32[16,256]{1,0:T(8,128)S(1)} %get-tuple-element.5.e32), custom_call_target="tpu_custom_call" | custom-call | tf_op jit(solution)/shard_map/write_out/pallas_call | solution.py:494

commit v6 on v5

--- a/solution.py
+++ b/solution.py
@@ -35,8 +35,8 @@
     hidden_hbm, queries_hbm, keys_hbm, values_hbm, lengths_hbm, weight_hbm, down_hbm, up_hbm, gain_hbm,
     o32, e32,
     hidden_v, queries_v, keys_v, values_v, lengths_s, weight_v, down_v, up_v, gain_v,
-    hf, rowf, q32, tiles, hall, wrap, bbuf, usend, urecv,
-    loc_sem, kv_sem, block_send, block_recv, quad_send, quad_recv, tile_send, tile_recv, b_sem, wrap_send, wrap_recv, u_send, u_recv,
+    hf, rowf, q32, acc32, top32, total32, tiles, hall, detour, bbuf, usend, urecv,
+    loc_sem, kv_sem, block_send, block_recv, quad_send, quad_recv, tile_send, tile_recv, b_sem, detour_send, detour_recv, u_send, u_recv,
 ):
     g = lax.axis_index("group")
     t = lax.axis_index("tp")
@@ -44,7 +44,6 @@
     z = zh * TP + t
     me = xy * 2 + c
     low, high = zh == 0, zh == 1
-    round_about = t >= TP - 2
 
     def at_z(where):
         return (xy * 4 + (where // TP) * 2 + c, where % TP)
@@ -91,7 +90,9 @@
         pl.semaphore_signal(barrier, inc=1, device_id=to, device_id_type=MESH)
 
     def greet_z(d):
-        greet(at_z((z - d + 2 * TP) % (2 * TP)))
+        @pl.when(jnp.logical_not(jnp.logical_and(z == TP, d == QUAD)))
+        def _():
+            greet(at_z((z - d + 2 * TP) % (2 * TP)))
 
         @pl.when(z + d < 2 * TP)
         def _():
@@ -103,14 +104,13 @@
     def _():
         greet(at_z(z + TP))
 
-    @pl.when(z == 0)
-    def _():
-        greet(at_z(TP - 2))
-        greet(at_z(TP - 1))
-
-    @pl.when(z >= 2 * TP - 2)
-    def _():
-        greet(at_z(0))
+    @pl.when(jnp.logical_or(z == 5, z == 12))
+    def _():
+        greet(at_z(z - 5))
+
+    @pl.when(z >= TP + 5)
+    def _():
+        greet(at_z(z - TP))
 
     times(0, PLANE - 1, lambda i: greet(in_plane(i)))
 
@@ -145,7 +145,7 @@
 
     @pl.when(low)
     def _():
-        extra = jnp.where(t == 0, 2, jnp.where(round_about, 1, 0))
+        extra = jnp.where(t == 4, -1, jnp.where(t == 7, 2, jnp.where(jnp.logical_or(t == 0, t > 4), 1, 0)))
         pl.semaphore_wait(barrier, PLANE - 1 + QUAD + jnp.minimum(t, QUAD) + extra)
 
     @pl.when(high)
@@ -154,10 +154,11 @@
 
     first_quad = t < QUAD
     above, below = (z + QUAD) % (2 * TP), (z + 2 * TP - QUAD) % (2 * TP)
-    sends_up = jnp.logical_or(jnp.logical_and(low, jnp.logical_not(round_about)), jnp.logical_and(high, first_quad))
+    sends_up = first_quad
     sends_down = jnp.logical_not(first_quad)
-    passes_low = jnp.logical_and(low, sends_down)
-    passes_high = jnp.logical_and(high, t < TP - 2 - QUAD)
+    passes = jnp.logical_and(z >= 5, z < TP)
+    detours = jnp.logical_and(low, t % 4 == 0)
+    direct = jnp.logical_and(low, t > 4)
 
     def up_copy():
         return remote(hall.at[z], hall.at[z], block_send.at[0], block_recv.at[0], at_z(above))
@@ -169,11 +170,20 @@
     def pass_copy():
         return remote(hall.at[below], hall.at[below], block_send.at[2], block_recv.at[2], at_z(above))
 
-    def round_copy():
-        return remote(hall.at[z], wrap.at[t - (TP - 2)], wrap_send.at[0], wrap_recv.at[t - (TP - 2)], at_z(0))
-
-    def wrap_copy(i):
-        return remote(wrap.at[i], hall.at[TP - 2 + i], wrap_send.at[i], block_recv.at[2], at_z(2 * TP - 2 + i))
+    def direct_copy():
+        return remote(hall.at[z], hall.at[z], block_send.at[0], block_recv.at[2], at_z((z + TP) % (2 * TP)))
+
+    def detour_copy():
+        to = jnp.where(t == 0, 5, 7)
+        return remote(hall.at[z], detour, detour_send.at[0], detour_recv, at_z(to))
+
+    def detour_on():
+        owner = jnp.where(t == 5, 0, 4)
+        return remote(detour, hall.at[owner], detour_send.at[1], block_recv.at[2], at_z(owner + TP))
+
+    def send_on():
+        wait_bytes(detour, detour_recv)
+        detour_on().start()
 
     def from_below():
         wait_bytes(hall.at[below], block_recv.at[0])
@@ -209,11 +219,15 @@
 
     @pl.when(low)
     def _():
-        @pl.when(round_about)
-        def _():
-            round_copy().start()
-
-        @pl.when(jnp.logical_not(round_about))
+        @pl.when(detours)
+        def _():
+            detour_copy().start()
+
+        @pl.when(direct)
+        def _():
+            direct_copy().start()
+
+        @pl.when(sends_up)
         def _():
             up_copy().start()
 
@@ -229,10 +243,21 @@
         def _():
             from_above()
 
+        @pl.when(t == 7)
+        def _():
+            send_on()
+
         @pl.when(jnp.logical_not(first_quad))
         def _():
             from_below()
-            pass_copy().start()
+
+            @pl.when(passes)
+            def _():
+                pass_copy().start()
+
+        @pl.when(t == 5)
+        def _():
+            send_on()
 
         times(0, QUAD - 1, lambda j: quad_copy(1, j).start())
 
@@ -240,20 +265,9 @@
     def _():
         send_down()
 
-    @pl.when(passes_high)
-    def _():
-        from_below()
-        pass_copy().start()
-
     @pl.when(jnp.logical_and(high, first_quad))
     def _():
         up_copy().start()
-
-    @pl.when(z == 0)
-    def _():
-        for i in (0, 1):
-            wait_bytes(wrap.at[i], wrap_recv.at[i])
-            wrap_copy(i).start()
 
     def rows_of(which, k):
         return tiles[which, :, k, :].astype(BF)
@@ -319,21 +333,20 @@
     factor = HEAD ** (-0.5)
 
     def cached(r):
-        kv[r][0].wait()
-        q = q32[r * QUERIES : (r + 1) * QUERIES, :].astype(BF)
-        scores = dot_t(q, keys_v[r]) * factor
+        wait_bytes(keys_v.at[r], kv_sem.at[0, r])
+        own = pl.ds(pl.multiple_of(r * QUERIES, QUERIES), QUERIES)
+        scores = dot_t(q32[own, :].astype(BF), keys_v[r]) * factor
         slot = lax.broadcasted_iota(jnp.int32, scores.shape, 1)
         scores = jnp.where(slot < lengths_s[r], scores, -jnp.inf)
         top = jnp.max(scores, axis=1, keepdims=True)
         p = jnp.exp(scores - top)
         total = jnp.sum(p, axis=1, keepdims=True)
-        kv[r][1].wait()
-        return top, total, dot(p.astype(BF), values_v[r])
-
-    rows = [cached(r) for r in range(ROWS)]
-    top_c = jnp.concatenate([r[0] for r in rows], axis=0)
-    total_c = jnp.concatenate([r[1] for r in rows], axis=0)
-    acc_c = jnp.concatenate([r[2] for r in rows], axis=0)
+        wait_bytes(values_v.at[r], kv_sem.at[1, r])
+        acc32[own, :] = dot(p.astype(BF), values_v[r])
+        top32[own, :] = jnp.broadcast_to(top, (QUERIES, HEAD))
+        total32[own, :] = jnp.broadcast_to(total, (QUERIES, HEAD))
+
+    times(0, ROWS, cached)
 
     @pl.when(high)
     def _():
@@ -356,9 +369,12 @@
     for which in range(2):
         times(0, QUAD - 1, lambda j, which=which: quad_arrived(which, j))
     small[6].wait()
-    base = jnp.zeros((TOKENS, 2 * HEAD), F32)
-    for i in range(TP):
-        base = base + dot(block_of(zh * TP + i), weight_v[i * KB * HEAD : (i + 1) * KB * HEAD, :])
+
+    def project(i, sofar):
+        depth = KB * HEAD
+        return sofar + dot(block_of(zh * TP + i), weight_v[pl.ds(pl.multiple_of(i * depth, depth), depth), :])
+
+    base = lax.fori_loop(0, TP, project, jnp.zeros((TOKENS, 2 * HEAD), F32))
     small[5].wait()
     gain = gain_v[...].reshape(1, HEAD)
 
@@ -395,11 +411,13 @@
     ki = lax.broadcasted_iota(jnp.int32, scores.shape, 1)
     seen = (ki % ROWS == qi // QUERIES) & (ki // ROWS <= (qi % QUERIES) // HEADS)
     scores = jnp.where(seen, scores, -jnp.inf)
+    top_c = top32[:, 0:1]
     top = jnp.maximum(top_c, jnp.max(scores, axis=1, keepdims=True))
     p = jnp.exp(scores - top)
     carry = jnp.exp(top_c - top)
-    total = carry * total_c + jnp.sum(p, axis=1, keepdims=True)
-    o32[...] = (carry * acc_c + dot(p.astype(BF), value.astype(BF))) / total
+    total = carry * total32[:, 0:1] + jnp.sum(p, axis=1, keepdims=True)
+    o32[...] = (carry * acc32[...] + dot(p.astype(BF), value.astype(BF))) / total
+
     @pl.when(sends_up)
     def _():
         up_copy().wait_send()
@@ -408,18 +426,21 @@
     def _():
         down_copy().wait_send()
 
-    @pl.when(jnp.logical_or(passes_low, passes_high))
+    @pl.when(passes)
     def _():
         pass_copy().wait_send()
 
-    @pl.when(jnp.logical_and(low, round_about))
-    def _():
-        round_copy().wait_send()
-
-    @pl.when(z == 0)
-    def _():
-        wrap_copy(0).wait_send()
-        wrap_copy(1).wait_send()
+    @pl.when(detours)
+    def _():
+        detour_copy().wait_send()
+
+    @pl.when(jnp.logical_or(z == 5, z == 7))
+    def _():
+        detour_on().wait_send()
+
+    @pl.when(direct)
+    def _():
+        direct_copy().wait_send()
 
     for which in range(2):
         times(0, QUAD - 1, lambda j, which=which: quad_copy(which, j).wait_send())
@@ -467,9 +488,12 @@
             pltpu.VMEM((TOKENS, KB * HEAD), F32),
             pltpu.VMEM((TOKENS, HEAD), F32),
             pltpu.VMEM((ROWS * QUERIES, HEAD), F32),
+            pltpu.VMEM((ROWS * QUERIES, HEAD), F32),
+            pltpu.VMEM((ROWS * QUERIES, HEAD), F32),
+            pltpu.VMEM((ROWS * QUERIES, HEAD), F32),
             pltpu.VMEM((2, PLANE, 8, HEAD), F32),
             pltpu.VMEM((2 * TP, KB + 1, TOKENS, HEAD), BF),
-            pltpu.VMEM((2, KB + 1, TOKENS, HEAD), BF),
+            pltpu.VMEM((KB + 1, TOKENS, HEAD), BF),
             pltpu.VMEM((2, PLANE, 2 * HEAD), BF),
             pltpu.VMEM((TOKENS, HEAD), BF),
             pltpu.VMEM((2, TP, TOKENS, HEAD), BF),
@@ -483,7 +507,7 @@
             dma((2,)),
             dma((2,)),
             dma((2,)),
-            dma((2,)),
+            dma,
             dma((3,)),
             dma((2,)),
         ],

time: 31.8 us -> 31.1 us (0.978)
  the two profiles are of different devices: /device:TPU:48 before, /device:TPU:1 now
where the time goes in v6:
time: 31.1 us; the launch traced here: 30.6 us
  Pallas kernels  30 us (96%)
  between operations  0.64 us (2%)
    pallas_call x1, Pallas kernels, per_device(): pl.pallas_call(kernel, name='decode', out_shape=(pltpu.VMEM((ROWS * QUERI...  29.3 us
    pallas_call x1, Pallas kernels, per_device(): pl.pallas_call(write_out, name='write_out', out_shape=(jax.ShapeDtypeStru...  0.67 us

profile of v6, /device:TPU:1, one launch (start us, length us, event | category | flops | bytes accessed | tf_op | source)
XLA Modules:
  0.0 30.6 jit_solution(6180582029932570536)
XLA Ops:
  0.6 29.3 %decode.1 = (f32[128,128]{1,0:T(8,128)S(1)}, f32[16,256]{1,0:T(8,128)S(1)}) custom-call(bf16[4,4,640]{2,1,0:T(4,128)(2,1)} %hidden_hbm.1, bf16[4,4,1024]{2,1,0:T(4,128)(2,1)} %queries_hbm.1, bf16[4,1024,128]{2,1,0:T(8,128)(2,1)} %keys_hbm.1, bf16[4,1024,128]{2,1,0:T(8,128)(2,1)} %values_hbm.1, s32[4]{0:T(128)} %lengths_hbm.1, bf16[5120,256]{1,0:T(8,128)(2,1)} %weight_hbm.1, ...), custom_call_target="tpu_custom_call" | custom-call | tf_op jit(solution)/shard_map/decode/pallas_call | solution.py:469
  30.0 0.7 %write_out.1 = (bf16[4,4,1024]{2,1,0:T(4,128)(2,1)}, bf16[4,4,256]{2,1,0:T(4,128)(2,1)}) custom-call(f32[128,128]{1,0:T(8,128)S(1)} %get-tuple-element.4.o32, f32[16,256]{1,0:T(8,128)S(1)} %get-tuple-element.5.e32), custom_call_target="tpu_custom_call" | custom-call | tf_op jit(solution)/shard_map/write_out/pallas_call | solution.py:518

commit v7 on v6

--- a/solution.py
+++ b/solution.py
@@ -81,39 +81,37 @@
             )
         )
     ]
+
+    barrier = pltpu.get_barrier_semaphore()
+
+    def greet(to):
+        pl.semaphore_signal(barrier, inc=1, device_id=to, device_id_type=MESH)
+
+    def greet_z(d):
+        greet(at_z((z - d + 2 * TP) % (2 * TP)))
+
+        @pl.when(z + d < 2 * TP)
+        def _():
+            greet(at_z(z + d))
+
+    times(1, QUAD + 1, greet_z)
+
+    @pl.when(low)
+    def _():
+        greet(at_z(z + TP))
+
+    @pl.when(z == 12)
+    def _():
+        greet(at_z(7))
+
+    @pl.when(z >= TP + 5)
+    def _():
+        greet(at_z(5))
+
+    times(0, PLANE - 1, lambda i: greet(in_plane(i)))
+
     for copy in small[:6]:
         copy.start()
-
-    barrier = pltpu.get_barrier_semaphore()
-
-    def greet(to):
-        pl.semaphore_signal(barrier, inc=1, device_id=to, device_id_type=MESH)
-
-    def greet_z(d):
-        @pl.when(jnp.logical_not(jnp.logical_and(z == TP, d == QUAD)))
-        def _():
-            greet(at_z((z - d + 2 * TP) % (2 * TP)))
-
-        @pl.when(z + d < 2 * TP)
-        def _():
-            greet(at_z(z + d))
-
-    times(1, QUAD + 1, greet_z)
-
-    @pl.when(low)
-    def _():
-        greet(at_z(z + TP))
-
-    @pl.when(jnp.logical_or(z == 5, z == 12))
-    def _():
-        greet(at_z(z - 5))
-
-    @pl.when(z >= TP + 5)
-    def _():
-        greet(at_z(z - TP))
-
-    times(0, PLANE - 1, lambda i: greet(in_plane(i)))
-
     kv = []
     for r in range(ROWS):
         kv.append(
@@ -140,12 +138,13 @@
         rowf[k : k + 1, :] = down[:, k * HEAD : (k + 1) * HEAD]
     for k in range(2):
         rowf[KB + k : KB + k + 1, :] = up[:, k * HEAD : (k + 1) * HEAD]
-    tiles[0, me] = rowf[0:8, :]
+    mine = pl.ds(pl.multiple_of(me * 8, 8), 8)
+    tiles[0, mine, :] = rowf[0:8, :]
     hall[z, KB] = rowf[...].astype(BF)
 
     @pl.when(low)
     def _():
-        extra = jnp.where(t == 4, -1, jnp.where(t == 7, 2, jnp.where(jnp.logical_or(t == 0, t > 4), 1, 0)))
+        extra = jnp.where(t == 5, 3, jnp.where(t == 7, 1, 0))
         pl.semaphore_wait(barrier, PLANE - 1 + QUAD + jnp.minimum(t, QUAD) + extra)
 
     @pl.when(high)
@@ -156,9 +155,9 @@
     above, below = (z + QUAD) % (2 * TP), (z + 2 * TP - QUAD) % (2 * TP)
     sends_up = first_quad
     sends_down = jnp.logical_not(first_quad)
-    passes = jnp.logical_and(z >= 5, z < TP)
-    detours = jnp.logical_and(low, t % 4 == 0)
-    direct = jnp.logical_and(low, t > 4)
+    passes = jnp.logical_and(low, sends_down)
+    detours = jnp.logical_and(low, jnp.logical_and(t >= 4, t != 5))
+    direct = z == 5
 
     def up_copy():
         return remote(hall.at[z], hall.at[z], block_send.at[0], block_recv.at[0], at_z(above))
@@ -174,16 +173,16 @@
         return remote(hall.at[z], hall.at[z], block_send.at[0], block_recv.at[2], at_z((z + TP) % (2 * TP)))
 
     def detour_copy():
-        to = jnp.where(t == 0, 5, 7)
-        return remote(hall.at[z], detour, detour_send.at[0], detour_recv, at_z(to))
-
-    def detour_on():
-        owner = jnp.where(t == 5, 0, 4)
-        return remote(detour, hall.at[owner], detour_send.at[1], block_recv.at[2], at_z(owner + TP))
-
-    def send_on():
-        wait_bytes(detour, detour_recv)
-        detour_on().start()
+        slot = jnp.where(t == 7, 1, 0)
+        to = jnp.where(t == 4, 7, 5)
+        return remote(hall.at[z], detour.at[slot], detour_send.at[2], detour_recv.at[slot], at_z(to))
+
+    def detour_on(slot, owner):
+        return remote(detour.at[slot], hall.at[owner], detour_send.at[slot], block_recv.at[2], at_z(owner + TP))
+
+    def send_on(slot, owner):
+        wait_bytes(detour.at[slot], detour_recv.at[slot])
+        detour_on(slot, owner).start()
 
     def from_below():
         wait_bytes(hall.at[below], block_recv.at[0])
@@ -206,7 +205,7 @@
 
     def tile_copy(which, i):
         return remote(
-            tiles.at[which, me], tiles.at[which, me], tile_send.at[which], tile_recv.at[which], in_plane(i)
+            tiles.at[which, mine], tiles.at[which, mine], tile_send.at[which], tile_recv.at[which], in_plane(i)
         )
 
     def send_down():
@@ -231,36 +230,33 @@
         def _():
             up_copy().start()
 
+    times(0, PLANE - 1, lambda i: tile_copy(0, i).start())
+
+    @pl.when(jnp.logical_and(low, first_quad))
+    def _():
+        times(0, QUAD - 1, lambda j: quad_copy(0, j).start())
+        from_above()
+        times(0, QUAD - 1, lambda j: quad_copy(1, j).start())
+
+    @pl.when(jnp.logical_and(low, jnp.logical_not(first_quad)))
+    def _():
+        @pl.when(t == 7)
+        def _():
+            send_on(0, 4)
+
+        from_below()
+
+        @pl.when(passes)
+        def _():
+            pass_copy().start()
+
+        @pl.when(t == 5)
+        def _():
+            send_on(0, 6)
+            send_on(1, 7)
+
         send_down()
 
-    times(0, PLANE - 1, lambda i: tile_copy(0, i).start())
-
-    @pl.when(low)
-    def _():
-        times(0, QUAD - 1, lambda j: quad_copy(0, j).start())
-
-        @pl.when(first_quad)
-        def _():
-            from_above()
-
-        @pl.when(t == 7)
-        def _():
-            send_on()
-
-        @pl.when(jnp.logical_not(first_quad))
-        def _():
-            from_below()
-
-            @pl.when(passes)
-            def _():
-                pass_copy().start()
-
-        @pl.when(t == 5)
-        def _():
-            send_on()
-
-        times(0, QUAD - 1, lambda j: quad_copy(1, j).start())
-
     @pl.when(high)
     def _():
         send_down()
@@ -270,7 +266,7 @@
         up_copy().start()
 
     def rows_of(which, k):
-        return tiles[which, :, k, :].astype(BF)
+        return tiles[which, pl.ds(k, PLANE, stride=8), :].astype(BF)
 
     def factor_of(which):
         return jnp.concatenate(
@@ -293,35 +289,6 @@
 
     def u_copy(src, which, where, send, to):
         return remote(src, urecv.at[which, where], u_send.at[send], u_recv.at[which], to)
-
-    wait_bytes(tiles.at[0, pl.ds(0, PLANE - 1)], tile_recv.at[0])
-    a_own = factor_of(0)
-
-    for k in range(2):
-        bbuf[0, :, k * HEAD : (k + 1) * HEAD] = rows_of(0, KB + k)
-
-    @pl.when(high)
-    def _():
-        b_copy().start()
-        wait_bytes(hall.at[t], block_recv.at[2])
-        usend[...] = parts(block_of(t), a_own)
-        times(0, TP, lambda i: u_copy(usend, 1, t, 1, (g - 2, i)).start())
-
-    @pl.when(high)
-    def _():
-        tiles[1, me] = hall[t, KB].astype(F32)[0:8]
-        times(0, PLANE - 1, lambda i: tile_copy(1, i).start())
-
-        times(0, QUAD - 1, lambda j: quad_copy(0, j).start())
-
-    urecv[0, t] = parts(block_of(z), a_own)
-
-    def own_copy(which, send, i):
-        return u_copy(urecv.at[which, t], which, t, send, (g, (t + 1 + i) % TP))
-
-    @pl.when(low)
-    def _():
-        times(0, TP - 1, lambda i: own_copy(0, 0, i).start())
 
     small[3].wait()
     for s in range(STEPS):
@@ -348,6 +315,41 @@
 
     times(0, ROWS, cached)
 
+    wait_bytes(tiles.at[0, pl.ds(0, 8 * PLANE - 8)], tile_recv.at[0])
+    a_own = factor_of(0)
+
+    for k in range(2):
+        bbuf[0, :, k * HEAD : (k + 1) * HEAD] = rows_of(0, KB + k)
+
+    @pl.when(high)
+    def _():
+        b_copy().start()
+        wait_bytes(hall.at[t], block_recv.at[2])
+
+        def rows_on():
+            tiles[1, mine, :] = hall[t, KB].astype(F32)[0:8]
+            times(0, PLANE - 1, lambda i: tile_copy(1, i).start())
+
+        pl.when(t >= 6)(rows_on)
+        usend[...] = parts(block_of(t), a_own)
+        times(0, TP, lambda i: u_copy(usend, 1, t, 1, (g - 2, i)).start())
+        pl.when(t < 6)(rows_on)
+        times(0, QUAD - 1, lambda j: quad_copy(0, j).start())
+
+    urecv[0, t] = parts(block_of(z), a_own)
+
+    def own_copy(which, send, i):
+        return u_copy(urecv.at[which, t], which, t, send, (g, (t + 1 + i) % TP))
+
+    @pl.when(low)
+    def _():
+        times(0, TP - 1, lambda i: own_copy(0, 0, i).start())
+
+    @pl.when(jnp.logical_and(low, jnp.logical_not(first_quad)))
+    def _():
+        times(0, QUAD - 1, lambda j: quad_copy(0, j).start())
+        times(0, QUAD - 1, lambda j: quad_copy(1, j).start())
+
     @pl.when(high)
     def _():
         @pl.when(first_quad)
@@ -360,7 +362,7 @@
 
         times(0, QUAD - 1, lambda j: quad_copy(1, j).start())
         times(0, TP - 1, lambda i: own_copy(0, 0, i).start())
-        wait_bytes(tiles.at[1, pl.ds(0, PLANE - 1)], tile_recv.at[1])
+        wait_bytes(tiles.at[1, pl.ds(0, 8 * PLANE - 8)], tile_recv.at[1])
         urecv[1, t] = parts(block_of(z), factor_of(1))
         times(0, TP - 1, lambda i: own_copy(1, 2, i).start())
         for k in range(2):
@@ -436,7 +438,11 @@
 
     @pl.when(jnp.logical_or(z == 5, z == 7))
     def _():
-        detour_on().wait_send()
+        detour_on(0, jnp.where(z == 5, 6, 4)).wait_send()
+
+    @pl.when(z == 5)
+    def _():
+        detour_on(1, 7).wait_send()
 
     @pl.when(direct)
     def _():
@@ -444,7 +450,7 @@
 
     for which in range(2):
         times(0, QUAD - 1, lambda j, which=which: quad_copy(which, j).wait_send())
-    wait_bytes(tiles.at[0, pl.ds(0, PLANE - 1)], tile_send.at[0])
+    wait_bytes(tiles.at[0, pl.ds(0, 8 * PLANE - 8)], tile_send.at[0])
     wait_bytes(urecv.at[0, pl.ds(0, TP - 1)], u_send.at[0])
 
     @pl.when(high)
@@ -452,7 +458,7 @@
         wait_bytes(urecv.at[1], u_send.at[1])
         wait_bytes(urecv.at[1, pl.ds(0, TP - 1)], u_send.at[2])
         b_copy().wait_send()
-        wait_bytes(tiles.at[1, pl.ds(0, PLANE - 1)], tile_send.at[1])
+        wait_bytes(tiles.at[1, pl.ds(0, 8 * PLANE - 8)], tile_send.at[1])
 
 
 def write_out(o32, e32, att_ref, ent_ref):
@@ -491,9 +497,9 @@
             pltpu.VMEM((ROWS * QUERIES, HEAD), F32),
             pltpu.VMEM((ROWS * QUERIES, HEAD), F32),
             pltpu.VMEM((ROWS * QUERIES, HEAD), F32),
-            pltpu.VMEM((2, PLANE, 8, HEAD), F32),
+            pltpu.VMEM((2, PLANE * 8, HEAD), F32),
             pltpu.VMEM((2 * TP, KB + 1, TOKENS, HEAD), BF),
-            pltpu.VMEM((KB + 1, TOKENS, HEAD), BF),
+            pltpu.VMEM((2, KB + 1, TOKENS, HEAD), BF),
             pltpu.VMEM((2, PLANE, 2 * HEAD), BF),
             pltpu.VMEM((TOKENS, HEAD), BF),
             pltpu.VMEM((2, TP, TOKENS, HEAD), BF),
@@ -506,8 +512,8 @@
             dma((2,)),
             dma((2,)),
             dma((2,)),
+            dma((3,)),
             dma((2,)),
-            dma,
             dma((3,)),
             dma((2,)),
         ],

time: 31.1 us -> 30.2 us (0.971)
  Pallas kernels: 30 us -> 29.4 us
    pallas_call x1, Pallas kernels: 29.3 us -> 28.7 us  [per_device(): pl.pallas_call(kernel, name='decode', out_shape=(pltpu.VMEM((ROWS * QUERI...]
where the time goes in v7:
time: 30.2 us; the launch traced here: 30 us
  Pallas kernels  29.4 us (97%)
  between operations  0.64 us (2%)
    pallas_call x1, Pallas kernels, per_device(): pl.pallas_call(kernel, name='decode', out_shape=(pltpu.VMEM((ROWS * QUERI...  28.7 us
    pallas_call x1, Pallas kernels, per_device(): pl.pallas_call(write_out, name='write_out', out_shape=(jax.ShapeDtypeStru...  0.67 us

profile of v7, /device:TPU:1, one launch (start us, length us, event | category | flops | bytes accessed | tf_op | source)
XLA Modules:
  0.0 30.0 jit_solution(9466466837126621912)
XLA Ops:
  0.6 28.7 %decode.1 = (f32[128,128]{1,0:T(8,128)S(1)}, f32[16,256]{1,0:T(8,128)S(1)}) custom-call(bf16[4,4,640]{2,1,0:T(4,128)(2,1)} %hidden_hbm.1, bf16[4,4,1024]{2,1,0:T(4,128)(2,1)} %queries_hbm.1, bf16[4,1024,128]{2,1,0:T(8,128)(2,1)} %keys_hbm.1, bf16[4,1024,128]{2,1,0:T(8,128)(2,1)} %values_hbm.1, s32[4]{0:T(128)} %lengths_hbm.1, bf16[5120,256]{1,0:T(8,128)(2,1)} %weight_hbm.1, ...), custom_call_target="tpu_custom_call" | custom-call | tf_op jit(solution)/shard_map/decode/pallas_call | solution.py:475
  29.4 0.7 %write_out.1 = (bf16[4,4,1024]{2,1,0:T(4,128)(2,1)}, bf16[4,4,256]{2,1,0:T(4,128)(2,1)}) custom-call(f32[128,128]{1,0:T(8,128)S(1)} %get-tuple-element.4.o32, f32[16,256]{1,0:T(8,128)S(1)} %get-tuple-element.5.e32), custom_call_target="tpu_custom_call" | custom-call | tf_op jit(solution)/shard_map/write_out/pallas_call | solution.py:524

commit v8 on v7

--- a/solution.py
+++ b/solution.py
@@ -235,8 +235,6 @@
     @pl.when(jnp.logical_and(low, first_quad))
     def _():
         times(0, QUAD - 1, lambda j: quad_copy(0, j).start())
-        from_above()
-        times(0, QUAD - 1, lambda j: quad_copy(1, j).start())
 
     @pl.when(jnp.logical_and(low, jnp.logical_not(first_quad)))
     def _():
@@ -315,6 +313,11 @@
 
     times(0, ROWS, cached)
 
+    @pl.when(jnp.logical_and(low, first_quad))
+    def _():
+        from_above()
+        times(0, QUAD - 1, lambda j: quad_copy(1, j).start())
+
     wait_bytes(tiles.at[0, pl.ds(0, 8 * PLANE - 8)], tile_recv.at[0])
     a_own = factor_of(0)
 
@@ -339,7 +342,7 @@
     urecv[0, t] = parts(block_of(z), a_own)
 
     def own_copy(which, send, i):
-        return u_copy(urecv.at[which, t], which, t, send, (g, (t + 1 + i) % TP))
+        return u_copy(urecv.at[which, t], which, t, send, (g, jnp.where(i < t, i, i + 1)))
 
     @pl.when(low)
     def _():

time: 30.2 us -> 30.2 us (level)
  no operation moved by 1% of the time
where the time goes in v8:
time: 30.2 us; the launch traced here: 30 us
  Pallas kernels  29.4 us (97%)
  between operations  0.64 us (2%)
    pallas_call x1, Pallas kernels, per_device(): pl.pallas_call(kernel, name='decode', out_shape=(pltpu.VMEM((ROWS * QUERI...  28.7 us
    pallas_call x1, Pallas kernels, per_device(): pl.pallas_call(write_out, name='write_out', out_shape=(jax.ShapeDtypeStru...  0.67 us

profile of v8, /device:TPU:1, one launch (start us, length us, event | category | flops | bytes accessed | tf_op | source)
XLA Modules:
  0.0 30.0 jit_solution(9700575830654966052)
XLA Ops:
  0.6 28.7 %decode.1 = (f32[128,128]{1,0:T(8,128)S(1)}, f32[16,256]{1,0:T(8,128)S(1)}) custom-call(bf16[4,4,640]{2,1,0:T(4,128)(2,1)} %hidden_hbm.1, bf16[4,4,1024]{2,1,0:T(4,128)(2,1)} %queries_hbm.1, bf16[4,1024,128]{2,1,0:T(8,128)(2,1)} %keys_hbm.1, bf16[4,1024,128]{2,1,0:T(8,128)(2,1)} %values_hbm.1, s32[4]{0:T(128)} %lengths_hbm.1, bf16[5120,256]{1,0:T(8,128)(2,1)} %weight_hbm.1, ...), custom_call_target="tpu_custom_call" | custom-call | tf_op jit(solution)/shard_map/decode/pallas_call | solution.py:478
  29.4 0.7 %write_out.1 = (bf16[4,4,1024]{2,1,0:T(4,128)(2,1)}, bf16[4,4,256]{2,1,0:T(4,128)(2,1)}) custom-call(f32[128,128]{1,0:T(8,128)S(1)} %get-tuple-element.4.o32, f32[16,256]{1,0:T(8,128)S(1)} %get-tuple-element.5.e32), custom_call_target="tpu_custom_call" | custom-call | tf_op jit(solution)/shard_map/write_out/pallas_call | solution.py:527
